TPU v7x, 32 devices: a whole 2x2x4 slice. The times are simulated.
32 devices in a mesh: dp: 4 (over y, x), mp: 8 (over z, core).
Axes of the slice: x: 2, y: 2, z: 4, core: 2. Of those that a mesh axis runs over, the one named last changes fastest.
Arguments:
- inputs: bfloat16 [8, 512, 8192], P('dp', 'mp'), may hold values from -6 to 6
- conditioning: bfloat16 [8, 8192, 80], P('dp', 'mp'), may hold values from -6 to 6
- lengths: int32 [8], P('dp'), may hold values from 2048 to 8192, as said below
- cotangent: bfloat16 [8, 2, 512, 8192], P('dp', None, 'mp'), may hold values from -6 to 6
- conv_weight: float32 [1104, 2, 512], P(None, None, 'mp'), may hold values from -0.1875 to 0.1875
- out_weight: float32 [512, 1024], P('mp'), may hold values from -0.75 to 0.75
- biases: float32 [4, 512], P(None, 'mp'), may hold values from -1.75 to 1.75
- conv_first: float32 [1104, 2, 512], P(None, None, 'mp'), may hold values from -1280 to 1280
- out_first: float32 [512, 1024], P('mp'), may hold values from -384 to 384
- bias_first: float32 [4, 512], P(None, 'mp'), may hold values from -1536 to 1536
- conv_second: float32 [1104, 2, 512], P(None, None, 'mp'), may hold values from 26214.4 to 419430.4
- out_second: float32 [512, 1024], P('mp'), may hold values from 1835.008 to 28835.84
- bias_second: float32 [4, 512], P(None, 'mp'), may hold values from 29491.2 to 471859.2
Outputs:
- layer_out: bfloat16 [8, 2, 512, 8192], P('dp', None, 'mp')
- grad_input: float32 [8, 512, 8192], P('dp', 'mp')
- grad_cond: float32 [8, 8192, 80], P('dp', 'mp')
- conv_weight_new: float32 [1104, 2, 512], P(None, None, 'mp')
- out_weight_new: float32 [512, 1024], P('mp')
- biases_new: float32 [4, 512], P(None, 'mp')
- conv_first_new: float32 [1104, 2, 512], P(None, None, 'mp')
- output_moment_renewed: float32 [512, 1024], P('mp')
- bias_first_new: float32 [4, 512], P(None, 'mp')
- conv_second_new: float32 [1104, 2, 512], P(None, None, 'mp')
- out_second_new: float32 [512, 1024], P('mp')
- bias_second_new: float32 [4, 512], P(None, 'mp')
- conv_weight_low: bfloat16 [1104, 2, 512], P(None, None, 'mp')
- out_weight_low: bfloat16 [512, 1024], P('mp')
- biases_low: bfloat16 [4, 512], P(None, 'mp')
Inputs may be any that keep to these rules, and one draw needn't show every extreme that they name: `lengths`: each clip's valid length; the first clip is full and the second has 2048 samples.
All inputs are finite; a program needn't handle non-finite values.
Results may differ from a plain program's by a relative error of at most 0.012.
Values may be sent and summed in bfloat16 or wider, within the bound.
A program may use at most 320 MiB of HBM per device.

v0:
```python
import jax
import jax.numpy as jnp
from jax import lax
from jax.sharding import PartitionSpec as P

RESIDUAL_WIDTH = 512
DILATION_STEP = 32
STEP = 4


BETA_ONE = 0.5
BETA_TWO = 0.5
EPSILON = 1e-08
WEIGHT_DECAY = 0.01
CONV_RATE = 0.03
OUT_RATE = 0.1
BIAS_RATE = 0.3


def delayed(value_array):
    pad_amount = jnp.zeros(value_array.shape[:-1] + (DILATION_STEP,), value_array.dtype)
    return jnp.concatenate([pad_amount, value_array[..., :-DILATION_STEP]], axis=-1)


def advanced(value_array):
    pad_amount = jnp.zeros(value_array.shape[:-1] + (DILATION_STEP,), value_array.dtype)
    return jnp.concatenate([value_array[..., DILATION_STEP:], pad_amount], axis=-1)


def validity(lengths, row_count):
    positions = lax.iota(jnp.int32, row_count)
    return (positions[None, :] < lengths[:, None]).astype(jnp.float32)


def conv_forward(delayed_tap, present_tap, condition, conv_low, bias_low):
    per_part = conv_low.shape[2]
    flat_weight = conv_low.reshape(conv_low.shape[0], 2 * per_part)
    pre_act = jnp.einsum(
        "crt,rk->ckt", delayed_tap, flat_weight[:RESIDUAL_WIDTH], preferred_element_type=jnp.float32
    )
    pre_act = pre_act + jnp.einsum(
        "crt,rk->ckt",
        present_tap,
        flat_weight[RESIDUAL_WIDTH : 2 * RESIDUAL_WIDTH],
        preferred_element_type=jnp.float32,
    )
    pre_act = pre_act + jnp.einsum(
        "ctm,mk->ckt",
        condition,
        flat_weight[2 * RESIDUAL_WIDTH :],
        preferred_element_type=jnp.float32,
    )
    shaped = pre_act.reshape(delayed_tap.shape[0], 2, per_part, delayed_tap.shape[2])
    return shaped + bias_low[None, :, :, None].astype(jnp.float32)


def gating(pre_act, keep_rows):
    tanh_part = jnp.tanh(pre_act[:, 0])
    sig_part = jax.nn.sigmoid(pre_act[:, 1])
    hidden = (keep_rows[:, None, :] * tanh_part * sig_part).astype(jnp.bfloat16)
    return (hidden, tanh_part, sig_part)


def gating_back(hidden_grad, tanh_part, sig_part, keep_rows):
    scaled = hidden_grad * keep_rows[:, None, :]
    tanh_grad = scaled * sig_part * (1.0 - tanh_part * tanh_part)
    sig_grad = scaled * tanh_part * sig_part * (1.0 - sig_part)
    return jnp.stack([tanh_grad, sig_grad], axis=1).astype(jnp.bfloat16)


def conv_backward(delayed_tap, present_tap, condition, conv_low, act_grad):
    flat_grad = act_grad.reshape(act_grad.shape[0], -1, act_grad.shape[3])
    flat_weight = conv_low.reshape(conv_low.shape[0], -1)
    back_earlier = jnp.einsum(
        "ckt,rk->crt", flat_grad, flat_weight[:RESIDUAL_WIDTH], preferred_element_type=jnp.float32
    )
    back_current = jnp.einsum(
        "ckt,rk->crt",
        flat_grad,
        flat_weight[RESIDUAL_WIDTH : 2 * RESIDUAL_WIDTH],
        preferred_element_type=jnp.float32,
    )
    back_cond = jnp.einsum(
        "ckt,mk->ctm",
        flat_grad,
        flat_weight[2 * RESIDUAL_WIDTH :],
        preferred_element_type=jnp.float32,
    )
    weight_grad = jnp.concatenate(
        [
            jnp.einsum("crt,ckt->rk", delayed_tap, flat_grad, preferred_element_type=jnp.float32),
            jnp.einsum("crt,ckt->rk", present_tap, flat_grad, preferred_element_type=jnp.float32),
            jnp.einsum("ctm,ckt->mk", condition, flat_grad, preferred_element_type=jnp.float32),
        ],
        axis=0,
    )
    return (back_earlier, back_current, back_cond, weight_grad.reshape(conv_low.shape))


def adamw(master, first_old, second_old, gradient, step_rate, power_one, power_two):
    first_new = BETA_ONE * first_old + (1.0 - BETA_ONE) * gradient
    second_new = BETA_TWO * second_old + (1.0 - BETA_TWO) * gradient * gradient
    first_hat = first_new / (1.0 - power_one)
    second_hat = second_new / (1.0 - power_two)
    renewed = master - step_rate * (
        first_hat / (jnp.sqrt(second_hat) + EPSILON) + WEIGHT_DECAY * master
    )
    return (renewed, first_new, second_new)


def per_device(
    inputs,
    conditioning,
    lengths,
    cotangent,
    conv_weight,
    out_weight,
    biases,
    conv_first,
    out_first,
    bias_first,
    conv_second,
    out_second,
    bias_second,
):
    clip_count = inputs.shape[0]
    slot_len = inputs.shape[2]
    conv_low = conv_weight.astype(jnp.bfloat16)
    out_low = out_weight.astype(jnp.bfloat16)
    bias_low = biases.astype(jnp.bfloat16)
    residual_back = cotangent[:, 0].astype(jnp.float32)
    present_tap, condition = (
        lax.all_gather(inputs, "mp", axis=1, tiled=True),
        lax.all_gather(conditioning, "mp", axis=1, tiled=True),
    )
    delayed_tap = delayed(present_tap)
    keep_rows = validity(lengths, slot_len)
    pre_act = conv_forward(delayed_tap, present_tap, condition, conv_low, bias_low[0:2])
    hidden, tanh_part, sig_part = gating(pre_act, keep_rows)
    partial_value = jnp.einsum(
        "ckt,kj->cjt", hidden, out_low, preferred_element_type=jnp.float32
    ).reshape(clip_count, 2, -1, slot_len)
    summed = lax.psum_scatter(partial_value, "mp", scatter_dimension=2, tiled=True)
    bias_out = bias_low[2:4].astype(jnp.float32)
    layer_out = jnp.stack(
        [
            inputs.astype(jnp.float32) + summed[:, 0] + bias_out[0][None, :, None],
            summed[:, 1] + bias_out[1][None, :, None],
        ],
        axis=1,
    ).astype(jnp.bfloat16)
    wide_back = lax.all_gather(cotangent, "mp", axis=2, tiled=True).reshape(
        clip_count, -1, slot_len
    )
    hidden_grad = jnp.einsum("cjt,kj->ckt", wide_back, out_low, preferred_element_type=jnp.float32)
    act_grad = gating_back(hidden_grad, tanh_part, sig_part, keep_rows)
    back_earlier, back_current, back_cond, conv_grad = conv_backward(
        delayed_tap, present_tap, condition, conv_low, act_grad
    )
    input_part = back_current + advanced(back_earlier)
    input_sum, grad_cond = (
        lax.psum_scatter(input_part, "mp", scatter_dimension=1, tiled=True),
        lax.psum_scatter(back_cond, "mp", scatter_dimension=1, tiled=True),
    )
    grad_input = residual_back + input_sum
    out_grad = jnp.einsum("ckt,cjt->kj", hidden, wide_back, preferred_element_type=jnp.float32)
    bias_grad = jnp.concatenate(
        [
            jnp.sum(act_grad.astype(jnp.float32), axis=(0, 3)),
            jnp.sum(cotangent.astype(jnp.float32), axis=(0, 3)),
        ],
        axis=0,
    )
    conv_grad, out_grad, bias_grad = (
        lax.psum(conv_grad.astype(jnp.bfloat16), "dp").astype(jnp.float32),
        lax.psum(out_grad.astype(jnp.bfloat16), "dp").astype(jnp.float32),
        lax.psum(bias_grad.astype(jnp.bfloat16), "dp").astype(jnp.float32),
    )
    power_one = jnp.float32(BETA_ONE**STEP)
    power_two = jnp.float32(BETA_TWO**STEP)
    conv_new = adamw(
        conv_weight, conv_first, conv_second, conv_grad, CONV_RATE, power_one, power_two
    )
    out_new = adamw(out_weight, out_first, out_second, out_grad, OUT_RATE, power_one, power_two)
    bias_new = adamw(biases, bias_first, bias_second, bias_grad, BIAS_RATE, power_one, power_two)
    return (
        layer_out,
        grad_input,
        grad_cond,
        conv_new[0],
        out_new[0],
        bias_new[0],
        conv_new[1],
        out_new[1],
        bias_new[1],
        conv_new[2],
        out_new[2],
        bias_new[2],
        conv_new[0].astype(jnp.bfloat16),
        out_new[0].astype(jnp.bfloat16),
        bias_new[0].astype(jnp.bfloat16),
    )


def solution(mesh):
    in_specs = (
        P("dp", "mp", None),
        P("dp", "mp", None),
        P("dp"),
        P("dp", None, "mp", None),
        P(None, None, "mp"),
        P("mp", None),
        P(None, "mp"),
        P(None, None, "mp"),
        P("mp", None),
        P(None, "mp"),
        P(None, None, "mp"),
        P("mp", None),
        P(None, "mp"),
    )
    out_specs = (
        P("dp", None, "mp", None),
        P("dp", "mp", None),
        P("dp", "mp", None),
        P(None, None, "mp"),
        P("mp", None),
        P(None, "mp"),
        P(None, None, "mp"),
        P("mp", None),
        P(None, "mp"),
        P(None, None, "mp"),
        P("mp", None),
        P(None, "mp"),
        P(None, None, "mp"),
        P("mp", None),
        P(None, "mp"),
    )
    return jax.shard_map(
        per_device, mesh=mesh, in_specs=in_specs, out_specs=out_specs, check_vma=False
    )
```

profile of v0, /device:TPU:0, one launch (start us, length us, event | category | flops | bytes accessed | tf_op | source)
XLA Modules:
  0.0 2015.8 jit_solution(442137741383269740)
XLA Ops:
  10.3 153.2 %all-gather.4.cloned.1.call-done = bf16[2,512,8192]{2,1,0:T(8,128)(2,1)} async-done(((bf16[2,64,8192]{2,1,0:T(8,128)(2,1)}), bf16[2,512,8192]{2,1,0:T(8,128)(2,1)}) %all-gather.4.cloned.1.call-update) | async-done | bytes 16777232 | tf_op jit(solution)/shard_map/all_gather | solution.py:133
  163.5 9.0 fusion.4
  172.5 11.5 fusion.8
  184.0 13.2 all-gather.6.cloned.1.call-done
  197.2 5.4 fusion.7
  202.6 5.3 copy_add_fusion
  207.9 278.6 %all-gather.8.cloned.1.call-done = bf16[2,2,512,8192]{3,2,1,0:T(8,128)(2,1)} async-done(((bf16[2,2,64,8192]{3,2,1,0:T(8,128)(2,1)}), bf16[2,2,512,8192]{3,2,1,0:T(8,128)(2,1)}) %all-gather.8.cloned.1.call-update) | async-done | bytes 33554448 | tf_op jit(solution)/shard_map/all_gather | solution.py:152
  486.5 17.9 fusion.41
  504.3 18.3 fusion.19
  522.6 2.7 fusion.70
  525.7 1.7 copy-done
  527.4 13.1 convolution_bitcast_fusion
  540.5 10.6 fusion.38
  551.2 8.7 fusion.44
  562.5 23.1 %slice.79 = f32[2,512,8160]{1,2,0:T(8,128)} slice(f32[2,512,8192]{1,2,0:T(8,128)} %convolution_bitcast_fusion), slice={[0:2], [0:512], [32:8192]} | slice | bytes 66846720 | tf_op jit(solution)/shard_map/slice | solution.py:27
  585.7 22.9 %bitcast_add_fusion = f32[2,512,8192]{1,2,0:T(8,128)} fusion(f32[2,512,8160]{1,2,0:T(8,128)} %slice.79, bf16[2,2,64,8192]{3,2,0,1:T(8,128)(2,1)} %copy-done, bf16[1104,2,64]{0,2,1:T(8,128)(2,1)S(1)} %copy-done.4), kind=kOutput, calls=%fused_computation | convolution fusion | flops 2155872256 | bytes 71303168 | tf_op jit(solution)/shard_map/ckt,rk->crt/dot_general | solution.py:77
  608.6 49.5 %copy.53 = f32[2,512,8192]{2,0,1:T(2,128)} copy(f32[2,512,8192]{1,2,0:T(8,128)} %bitcast_add_fusion) | data formatting | bytes 67108864 | tf_op jit(solution)/shard_map/add | solution.py:160
  658.1 27.2 %fusion.26 = f32[2,8192,1024]{1,2,0:T(8,128)} fusion(f32[2,2,64,8192]{3,2,0,1:T(8,128)} %copy_add_fusion, f32[2,8192]{1,0:T(2,128)S(1)} %compare_convert_fusion, f32[64,1024]{1,0:T(8,128)S(1)} %copy-done.7), kind=kOutput, calls=%fused_computation.45 | convolution fusion | flops 2153840640 | bytes 75825152 | tf_op jit(solution)/shard_map/ckt,kj->cjt/dot_general | solution.py:140
  685.4 5.5 convolution_bitcast_fusion.3
  691.0 1.8 slice.69
  692.8 3.4 reduce.1
  698.7 10.1 psum.23
  710.1 2.1 fusion.66
  712.3 2.7 fusion.68
  715.0 590.0 %all-reduce.7.cloned.1.call-done = f32[2,512,8192]{2,0,1:T(2,128)} async-done(((f32[2,512,8192]{2,0,1:T(2,128)}), f32[2,512,8192]{2,0,1:T(2,128)}) %all-reduce.7.cloned.1.call-update) | async-done | bytes 33554448
  1305.0 5.2 convert_add_fusion
  1310.2 4.4 copy.57
  1314.6 632.7 %reduce-scatter.3.cloned.1.call-done = f32[2,2,64,8192]{3,2,1,0:T(8,128)} async-done(((f32[2,2,512,8192]{3,2,1,0:T(8,128)}), f32[2,2,64,8192]{3,2,1,0:T(8,128)}) %reduce-scatter.3.cloned.1.call-update) | async-done | bytes 8388624 | tf_op jit(solution)/shard_map/reduce_scatter | solution.py:143
  1947.3 2.5 fusion.10
  1949.9 2.8 fusion.28
  1952.7 2.4 pad_maximum_fusion
  1955.1 53.4 %reduce-scatter.5.cloned.1.call-done = f32[2,1024,80]{1,2,0:T(8,128)} async-done(((f32[2,8192,80]{1,2,0:T(8,128)}), f32[2,1024,80]{1,2,0:T(8,128)}) %reduce-scatter.5.cloned.1.call-update) | async-done | bytes 655376 | tf_op jit(solution)/shard_map/reduce_scatter | solution.py:163
  (63 shorter events, 9.3 us)
Async XLA Ops:
  7.2 2.3 copy-start.5
  7.2 2.4 copy-start.9
  7.2 3.0 copy-start.15
  7.2 156.3 %all-gather.4.cloned.1.call-start = ((), (), s32[]{:S(2)}) async-start(), calls=%async_computation.2 | async-start | bytes 18874368 | tf_op jit(solution)/shard_map/all_gather | solution.py:133
  7.9 189.2 %all-gather.6.cloned.1.call-start = ((), (), s32[]{:S(2)}) async-start(), calls=%async_computation.3 | async-start | bytes 2949120 | tf_op jit(solution)/shard_map/all_gather | solution.py:134
  8.7 477.8 %all-gather.8.cloned.1.call-start = ((), (), s32[]{:S(2)}) async-start(), calls=%async_computation.5 | async-start | bytes 37748736 | tf_op jit(solution)/shard_map/all_gather | solution.py:152
  9.4 700.7 %all-reduce.9.cloned.1.call-start = ((), (), s32[]{:S(2)}) async-start(), calls=%async_computation.8 | async-start | bytes 851968 | tf_op jit(solution)/shard_map/psum | solution.py:175
  9.5 163.0 %copy-start.3 = (bf16[1104,2,64]{0,2,1:T(8,128)(2,1)}, bf16[1104,2,64]{0,2,1:T(8,128)(2,1)S(1)}, u32[]{:S(2)}) copy-start(bf16[1104,2,64]{0,2,1:T(8,128)(2,1)S(1)} %convert_element_type.82) | copy-start | bytes 847876
  172.5 24.7 %slice-start = ((bf16[1104,2,64]{0,2,1:T(8,128)(2,1)}), bf16[80,2,64]{0,2,1:T(8,128)(2,1)S(1)}, s32[]{:S(2)}) async-start(bf16[1104,2,64]{0,2,1:T(8,128)(2,1)} %copy-done.3), calls=%async_computation.9 | async-start | bytes 65536 | tf_op jit(solution)/shard_map/slice | solution.py:50
  486.5 17.9 copy-start.7
  525.4 2.0 copy-start
  525.4 2.0 copy-start.4
  551.1 8.7 copy-start.1
  585.6 719.4 %all-reduce.7.cloned.1.call-start = ((), (), s32[]{:S(2)}) async-start(), calls=%async_computation.7 | async-start | bytes 67108864
  658.1 1289.2 %reduce-scatter.3.cloned.1.call-start = ((), (), s32[]{:S(2)}) async-start(), calls=%async_computation.4 | async-start | bytes 75497472 | tf_op jit(solution)/shard_map/reduce_scatter | solution.py:143
  685.4 1323.2 %reduce-scatter.5.cloned.1.call-start = ((), (), s32[]{:S(2)}) async-start(), calls=%async_computation.6 | async-start | bytes 5898240 | tf_op jit(solution)/shard_map/reduce_scatter | solution.py:163
  690.9 5.3 copy-start.16
  690.9 6.5 copy-start.11
  691.0 7.1 copy-start.12
  691.0 17.9 copy-start.10
  691.0 21.3 %copy-start.6 = (f32[1104,2,64]{0,2,1:T(8,128)S(1)}, f32[1104,2,64]{0,2,1:T(8,128)}, u32[]{:S(2)}) copy-start(f32[1104,2,64]{0,2,1:T(8,128)} %param.17) | copy-start | bytes 1695748
  691.0 21.3 %copy-start.8 = (f32[1104,2,64]{0,2,1:T(8,128)S(1)}, f32[1104,2,64]{0,2,1:T(8,128)}, u32[]{:S(2)}) copy-start(f32[1104,2,64]{0,2,1:T(8,128)} %param.20) | copy-start | bytes 1695748
  1310.2 637.1 %copy-start.14 = (f32[64]{0:T(128)S(1)}, f32[64]{0:T(128)}, u32[]{:S(2)}) copy-start(f32[64]{0:T(128)} %get-tuple-element.81) | copy-start | bytes 772
  1314.6 635.2 %copy-start.2 = (bf16[2,64,8192]{2,1,0:T(8,128)(2,1)S(1)}, bf16[2,64,8192]{2,1,0:T(8,128)(2,1)}, u32[]{:S(2)}) copy-start(bf16[2,64,8192]{2,1,0:T(8,128)(2,1)} %param.13) | copy-start | bytes 6291460
  1314.6 635.2 %copy-start.13 = (f32[64]{0:T(128)S(1)}, f32[64]{0:T(128)}, u32[]{:S(2)}) copy-start(f32[64]{0:T(128)} %get-tuple-element.80) | copy-start | bytes 772
Sparse Core Ops, SparseCore 0:
  9.7 153.7 all-gather.3
  165.1 32.0 all-gather.5
  198.8 287.6 all-gather.7
  585.8 42.7 all-reduce.8
  658.2 646.7 all-reduce.6
  1307.3 639.9 reduce-scatter.2
  1950.2 58.2 reduce-scatter.4
where the time goes:
time: 2020 us
  waiting for transfers between devices  1720 us (85%)
  matrix products  152 us (8%)
  local copies, waits for them, and re-layouts  83.1 us (4%)
  other arithmetic  31.9 us (2%)
    reduce_scatter x1, waiting for transfers between devices, per_device(): lax.psum_scatter(partial_value, 'mp', scatter_dimension=2, tiled=True)  633 us
    unnamed x8, waiting for transfers between devices  592 us
    all_gather x1, waiting for transfers between devices, per_device(): lax.all_gather(cotangent, 'mp', axis=2, tiled=True)  279 us
    all_gather x1, waiting for transfers between devices, per_device(): lax.all_gather(inputs, 'mp', axis=1, tiled=True)  153 us
    reduce_scatter x1, waiting for transfers between devices, per_device(): lax.psum_scatter(back_cond, 'mp', scatter_dimension=1, tiled=True)  53.4 us
    add x1, local copies, waits for them, and re-layouts, per_device(): input_part = back_current + advanced(back_earlier)  49.5 us
  transfers between devices with their start and end apart: 7, of which 6 were waited for; matrix products, arithmetic and copies ran while one was open for 8% of the time, Pallas kernels for 0%

commit v1 on v0

v1 whole, which is shorter than its diff:
```python
import functools

import jax
import jax.numpy as jnp
from jax import lax
from jax.experimental import pallas as pl
from jax.experimental.pallas import tpu as pltpu
from jax.sharding import PartitionSpec as P

RESIDUAL_WIDTH = 512
GH = 512
DILATION_STEP = 32
STEP = 4

BETA_ONE = 0.5
BETA_TWO = 0.5
EPSILON = 1e-08
WEIGHT_DECAY = 0.01
CONV_RATE = 0.03
OUT_RATE = 0.1
BIAS_RATE = 0.3

MESH = pl.DeviceIdType.MESH
LANES = 128
KP = 1152
OUT_AT = 2 * KP
SUM_AT = OUT_AT + 1024
WIDE = 3584
BF = jnp.bfloat16
F32 = jnp.float32


def dot(a, b):
    return jnp.dot(a, b, preferred_element_type=F32)


def dot_nt(a, b):
    return lax.dot_general(a, b, (((1,), (1,)), ((), ())), preferred_element_type=F32)


def layer_kernel(
    n, d, clips, slot, sub,
    x, cot, cnd, lens, wcat, bsum,
    bro, gio, halo, gct, gw,
    xin, cin, wall, wtr, pg, gacc, bst, gst, hst, s1, r1, s2, r2,
    sem_send, sem_x, sem_c, sem_w, sem_out, sem_r1, sem_r2,
):
    g = lax.axis_index("dp")
    m = lax.axis_index("mp")
    r = RESIDUAL_WIDTH // n
    t = slot // n
    piece = WIDE // d

    def peer(k):
        return lax.rem(m + k, n)

    def lane(i, size):
        return pl.ds(pl.multiple_of(i, LANES), size)

    def rows(j):
        return pl.ds(pl.multiple_of(j * r, r), r)

    def remote(src, dst, ss, rs, gg, j):
        return pltpu.make_async_remote_copy(
            src_ref=src, dst_ref=dst, send_sem=ss, recv_sem=rs,
            device_id=(gg, j), device_id_type=MESH,
        )

    def drain(ref, sem):
        pltpu.make_async_copy(ref, ref, sem).wait()

    bar = pltpu.get_barrier_semaphore()

    @pl.loop(1, n)
    def _(k):
        pl.semaphore_signal(bar, inc=1, device_id=(g, peer(k)), device_id_type=MESH)

    @pl.loop(1, d)
    def _(k):
        pl.semaphore_signal(bar, inc=1, device_id=(lax.rem(g + k, d), m), device_id_type=MESH)

    pl.semaphore_wait(bar, n + d - 2)

    mine = lane(g * piece, piece)

    @pl.loop(1, n)
    def _(k):
        remote(wcat.at[:, mine], wall.at[rows(m), mine], sem_send.at[0], sem_w.at[0], g, peer(k)).start()

    pltpu.make_async_copy(wcat.at[:, mine], wall.at[rows(m), mine], sem_w.at[0]).start()

    for c in range(clips):
        @pl.loop(1, n)
        def _(k):
            j = peer(k)
            remote(x.at[c, :, lane(j * t, t)], xin.at[c, rows(m), pl.ds(LANES, t)],
                   sem_send.at[1], sem_x.at[c], g, j).start()
            remote(x.at[c, :, lane(lax.rem(j * t + slot - LANES, slot), LANES)], xin.at[c, rows(m), pl.ds(0, LANES)],
                   sem_send.at[2], sem_x.at[c], g, j).start()
            remote(cot.at[c, :, :, lane(j * t, t)], cin.at[c, :, rows(m), :],
                   sem_send.at[3], sem_c.at[c], g, j).start()

        pltpu.make_async_copy(x.at[c, :, lane(m * t, t)], xin.at[c, rows(m), pl.ds(LANES, t)], sem_x.at[c]).start()
        pltpu.make_async_copy(x.at[c, :, lane(lax.rem(m * t + slot - LANES, slot), LANES)],
                              xin.at[c, rows(m), pl.ds(0, LANES)], sem_x.at[c]).start()
        pltpu.make_async_copy(cot.at[c, :, :, lane(m * t, t)], cin.at[c, :, rows(m), :], sem_c.at[c]).start()

    gacc[...] = jnp.zeros_like(gacc)
    gacc[rows(m), pl.ds(SUM_AT, LANES)] = bsum[...]
    pg[...] = jnp.zeros_like(pg)

    drain(wall.at[:, mine], sem_w.at[0])

    @pl.loop(1, d)
    def _(k):
        remote(wall.at[:, mine], wall.at[:, mine], sem_send.at[4], sem_w.at[1], lax.rem(g + k, d), m).start()

    drain(wall.at[:, pl.ds(0, (d - 1) * piece)], sem_w.at[1])

    @pl.loop(0, SUM_AT // LANES)
    def _(i):
        wtr[pl.ds(pl.multiple_of(i * LANES, LANES), LANES), :] = wall[:, lane(i * LANES, LANES)].T

    def clip(c):
        drain(xin.at[c], sem_x.at[c])

        @pl.when(m == 0)
        def _():
            xin[c, :, 0:LANES] = jnp.zeros((RESIDUAL_WIDTH, LANES), BF)

        drain(cin.at[c], sem_c.at[c])
        length = lens[c]

        @pl.loop(0, t // sub)
        def _(k):
            at = pl.multiple_of(k * sub, LANES)
            now = lane(at, sub)
            off = lane(at + LANES, sub)
            xc = xin[c, :, off]
            xe = pltpu.roll(xin[c, :, lane(at, sub + LANES)], DILATION_STEP, 1)[:, LANES:]
            cd = cnd[c, :, now]
            pre_f = (dot(wall[:, 0:512], xe) + dot(wall[:, 512:1024], xc) + dot(wall[:, 1024:KP], cd))
            pre_g = (dot(wall[:, KP:KP + 512], xe) + dot(wall[:, KP + 512:KP + 1024], xc)
                     + dot(wall[:, KP + 1024:OUT_AT], cd))
            place = m * t + at + lax.broadcasted_iota(jnp.int32, (1, sub), 1)
            keep = (place < length).astype(F32)
            th = jnp.tanh(pre_f)
            sg = jax.nn.sigmoid(pre_g)
            hid = (keep * th * sg).astype(BF)
            branch = dot(wtr[OUT_AT:SUM_AT, :], hid).astype(BF)
            bst[c, 0, :, now] = branch[0:512]
            bst[c, 1, :, now] = branch[512:1024]

            @pl.loop(1, n)
            def _(q):
                j = peer(q)
                remote(bst.at[c, :, rows(j), now], bro.at[c, :, :, lane(m * t + at, sub)],
                       sem_send.at[5], sem_out.at[0], g, j).start()

            pltpu.make_async_copy(bst.at[c, :, rows(m), now], bro.at[c, :, :, lane(m * t + at, sub)],
                                  sem_out.at[0]).start()
            ct = cin[c, :, :, now].reshape(1024, sub)
            hg = dot(wall[:, OUT_AT:SUM_AT], ct) * keep
            pgf = (hg * sg * (1.0 - th * th)).astype(BF)
            pgg = (hg * th * sg * (1.0 - sg)).astype(BF)
            pg[0:512, off] = pgf
            pg[512:1024, off] = pgg
            gacc[:, 0:512] += dot_nt(pgf, xe)
            gacc[:, 512:1024] += dot_nt(pgf, xc)
            gacc[:, 1024:KP] += dot_nt(pgf, cd)
            gacc[:, KP:KP + 512] += dot_nt(pgg, xe)
            gacc[:, KP + 512:KP + 1024] += dot_nt(pgg, xc)
            gacc[:, KP + 1024:OUT_AT] += dot_nt(pgg, cd)
            gacc[:, OUT_AT:SUM_AT] += dot_nt(hid, ct)
            gct[c, :, now] = dot(wtr[1024:KP, :], pgf) + dot(wtr[KP + 1024:OUT_AT, :], pgg)

        def back(off, size):
            win = pg[:, lane(off, size + LANES)]
            pn = win[:, :size]
            pe = pltpu.roll(win, size + LANES - DILATION_STEP, 1)[:, :size]
            return (dot(wtr[512:1024, :], pn[0:512]) + dot(wtr[KP + 512:KP + 1024, :], pn[512:1024])
                    + dot(wtr[0:512, :], pe[0:512]) + dot(wtr[KP:KP + 512, :], pe[512:1024]))

        hst[c] = back(0, LANES).astype(BF)

        @pl.loop(1, n)
        def _(q):
            j = peer(q)
            remote(hst.at[c, rows(j), :], halo.at[c, :, lane(m * LANES, LANES)],
                   sem_send.at[6], sem_out.at[1], g, j).start()

        pltpu.make_async_copy(hst.at[c, rows(m), :], halo.at[c, :, lane(m * LANES, LANES)], sem_out.at[1]).start()

        @pl.loop(0, t // sub)
        def _(k):
            at = pl.multiple_of(k * sub, LANES)
            now = lane(at, sub)
            gst[c, :, now] = back(at + LANES, sub).astype(BF)

            @pl.loop(1, n)
            def _(q):
                j = peer(q)
                remote(gst.at[c, rows(j), now], gio.at[c, :, lane(m * t + at, sub)],
                       sem_send.at[7], sem_out.at[2], g, j).start()

            pltpu.make_async_copy(gst.at[c, rows(m), now], gio.at[c, :, lane(m * t + at, sub)],
                                  sem_out.at[2]).start()

    pl.loop(0, clips)(clip)

    @pl.loop(1, d)
    def _(k):
        to = lax.rem(g + k, d)
        s1[k - 1] = gacc[:, lane(to * piece, piece)].astype(BF)
        remote(s1.at[k - 1], r1.at[k - 1], sem_send.at[8], sem_r1.at[k - 1], to, m).start()

    @pl.loop(1, d)
    def _(k):
        drain(r1.at[k - 1], sem_r1.at[k - 1])
        gacc[:, mine] += r1[k - 1].astype(F32)

    s2[...] = gacc[:, mine].astype(BF)

    @pl.loop(1, n)
    def _(k):
        j = peer(k)
        remote(s2.at[rows(j), :], r2.at[k - 1], sem_send.at[9], sem_r2.at[k - 1], g, j).start()

    gw[:, mine] = gacc[rows(m), mine]

    @pl.loop(1, n)
    def _(k):
        drain(r2.at[k - 1], sem_r2.at[k - 1])
        gw[:, mine] += r2[k - 1].astype(F32)

    @pl.loop(1, d)
    def _(k):
        remote(gw.at[:, mine], gw.at[:, mine], sem_send.at[10], sem_w.at[2], lax.rem(g + k, d), m).start()

    drain(gw.at[:, pl.ds(0, (d - 1) * piece)], sem_w.at[2])

    others = pl.ds(0, (n - 1) * r)
    drain(wall.at[others, pl.ds(0, piece)], sem_send.at[0])
    drain(x.at[:, :, pl.ds(0, (n - 1) * t)], sem_send.at[1])
    drain(halo.at[:, :, pl.ds(0, (n - 1) * LANES)], sem_send.at[2])
    drain(cot.at[:, :, :, pl.ds(0, (n - 1) * t)], sem_send.at[3])
    drain(wall.at[:, pl.ds(0, (d - 1) * piece)], sem_send.at[4])
    drain(bst.at[:, :, others, :], sem_send.at[5])
    drain(hst.at[:, others, :], sem_send.at[6])
    drain(gst.at[:, others, :], sem_send.at[7])
    drain(s1, sem_send.at[8])
    drain(s2.at[others, :], sem_send.at[9])
    drain(gw.at[:, pl.ds(0, (d - 1) * piece)], sem_send.at[10])
    drain(bro, sem_out.at[0])
    drain(halo, sem_out.at[1])
    drain(gio, sem_out.at[2])


def run_layer(n, d, x, cot, cnd, lens, wcat, bsum):
    clips, r, slot = x.shape
    t = slot // n
    sub = min(256, t)
    piece = WIDE // d
    width = RESIDUAL_WIDTH
    any_spec = pl.BlockSpec(memory_space=pl.ANY)
    vmem = pl.BlockSpec(memory_space=pltpu.VMEM)
    smem = pl.BlockSpec(memory_space=pltpu.SMEM)
    dma = pltpu.SemaphoreType.DMA
    return pl.pallas_call(
        functools.partial(layer_kernel, n, d, clips, slot, sub),
        out_shape=(
            jax.ShapeDtypeStruct((clips, 2, r, slot), BF),
            jax.ShapeDtypeStruct((clips, r, slot), BF),
            jax.ShapeDtypeStruct((clips, r, n * LANES), BF),
            jax.ShapeDtypeStruct((clips, LANES, t), F32),
            jax.ShapeDtypeStruct((r, WIDE), F32),
        ),
        in_specs=[any_spec, any_spec, vmem, smem, vmem, vmem],
        out_specs=(any_spec, any_spec, any_spec, vmem, vmem),
        scratch_shapes=[
            pltpu.VMEM((clips, width, LANES + t), BF),
            pltpu.VMEM((clips, 2, width, t), BF),
            pltpu.VMEM((GH, WIDE), BF),
            pltpu.VMEM((SUM_AT, GH), BF),
            pltpu.VMEM((2 * GH, t + 2 * LANES), BF),
            pltpu.VMEM((GH, WIDE), F32),
            pltpu.VMEM((clips, 2, width, t), BF),
            pltpu.VMEM((clips, width, t), BF),
            pltpu.VMEM((clips, width, LANES), BF),
            pltpu.VMEM((d - 1, GH, piece), BF),
            pltpu.VMEM((d - 1, GH, piece), BF),
            pltpu.VMEM((GH, piece), BF),
            pltpu.VMEM((n - 1, r, piece), BF),
            dma((11,)),
            dma((clips,)),
            dma((clips,)),
            dma((3,)),
            dma((3,)),
            dma((d - 1,)),
            dma((n - 1,)),
        ],
        compiler_params=pltpu.CompilerParams(
            collective_id=0, has_side_effects=True, vmem_limit_bytes=60 << 20
        ),
    )(x, cot, cnd, lens, wcat, bsum)


def adamw(master, first_old, second_old, gradient, step_rate, power_one, power_two):
    first_new = BETA_ONE * first_old + (1.0 - BETA_ONE) * gradient
    second_new = BETA_TWO * second_old + (1.0 - BETA_TWO) * gradient * gradient
    first_hat = first_new / (1.0 - power_one)
    second_hat = second_new / (1.0 - power_two)
    renewed = master - step_rate * (
        first_hat / (jnp.sqrt(second_hat) + EPSILON) + WEIGHT_DECAY * master
    )
    return (renewed, first_new, second_new)


def per_device(
    n, d,
    inputs, conditioning, lengths, cotangent, conv_weight, out_weight, biases,
    conv_first, out_first, bias_first, conv_second, out_second, bias_second,
):
    clips, r, slot = inputs.shape
    t = slot // n
    taps = conv_weight.shape[0]
    mel = conditioning.shape[2]
    bias_low = biases.astype(BF)
    flipped = jnp.transpose(conv_weight.astype(BF), (1, 2, 0))
    flipped = jnp.concatenate(
        [flipped, bias_low[0:2, :, None], jnp.zeros((2, r, KP - taps - 1), BF)], axis=2
    )
    wcat = jnp.concatenate(
        [flipped[0], flipped[1], out_weight.astype(BF), jnp.zeros((r, WIDE - SUM_AT), BF)], axis=1
    )
    cnd = jnp.concatenate(
        [
            jnp.transpose(conditioning, (0, 2, 1)),
            jnp.ones((clips, 1, t), BF),
            jnp.zeros((clips, LANES - mel - 1, t), BF),
        ],
        axis=1,
    )
    sums = jnp.sum(cotangent.astype(F32), axis=(0, 3))
    bsum = jnp.pad(sums.T, ((0, 0), (0, LANES - 2)))
    bro, gio, halo, gct, gw = run_layer(n, d, inputs, cotangent, cnd, lengths, wcat, bsum)

    bias_out = bias_low[2:4].astype(F32)
    layer_out = jnp.stack(
        [
            inputs.astype(F32) + bro[:, 0].astype(F32) + bias_out[0][None, :, None],
            bro[:, 1].astype(F32) + bias_out[1][None, :, None],
        ],
        axis=1,
    ).astype(BF)
    edge = halo.astype(F32).reshape(clips, r, n, LANES)
    edge = jnp.concatenate([edge[:, :, 1:], jnp.zeros((clips, r, 1, LANES), F32)], axis=2)
    edge = jnp.pad(edge, ((0, 0), (0, 0), (0, 0), (t - LANES, 0))).reshape(clips, r, slot)
    grad_input = cotangent[:, 0].astype(F32) + (gio.astype(F32) + edge)
    grad_cond = jnp.transpose(gct[:, :mel], (0, 2, 1))
    conv_grad = jnp.transpose(
        jnp.stack([gw[:, :taps], gw[:, KP : KP + taps]], axis=0), (2, 0, 1)
    )
    out_grad = gw[:, OUT_AT:SUM_AT]
    bias_grad = jnp.stack(
        [gw[:, taps], gw[:, KP + taps], gw[:, SUM_AT], gw[:, SUM_AT + 1]], axis=0
    )
    power_one = jnp.float32(BETA_ONE**STEP)
    power_two = jnp.float32(BETA_TWO**STEP)
    conv_new = adamw(
        conv_weight, conv_first, conv_second, conv_grad, CONV_RATE, power_one, power_two
    )
    out_new = adamw(out_weight, out_first, out_second, out_grad, OUT_RATE, power_one, power_two)
    bias_new = adamw(biases, bias_first, bias_second, bias_grad, BIAS_RATE, power_one, power_two)
    return (
        layer_out,
        grad_input,
        grad_cond,
        conv_new[0],
        out_new[0],
        bias_new[0],
        conv_new[1],
        out_new[1],
        bias_new[1],
        conv_new[2],
        out_new[2],
        bias_new[2],
        conv_new[0].astype(BF),
        out_new[0].astype(BF),
        bias_new[0].astype(BF),
    )


def solution(mesh):
    in_specs = (
        P("dp", "mp", None),
        P("dp", "mp", None),
        P("dp"),
        P("dp", None, "mp", None),
        P(None, None, "mp"),
        P("mp", None),
        P(None, "mp"),
        P(None, None, "mp"),
        P("mp", None),
        P(None, "mp"),
        P(None, None, "mp"),
        P("mp", None),
        P(None, "mp"),
    )
    out_specs = (
        P("dp", None, "mp", None),
        P("dp", "mp", None),
        P("dp", "mp", None),
        P(None, None, "mp"),
        P("mp", None),
        P(None, "mp"),
        P(None, None, "mp"),
        P("mp", None),
        P(None, "mp"),
        P(None, None, "mp"),
        P("mp", None),
        P(None, "mp"),
        P(None, None, "mp"),
        P("mp", None),
        P(None, "mp"),
    )
    return jax.shard_map(
        functools.partial(per_device, mesh.shape["mp"], mesh.shape["dp"]),
        mesh=mesh, in_specs=in_specs, out_specs=out_specs, check_vma=False,
    )
```

time: 2020 us -> 374 us (0.19)
  waiting for transfers between devices: 1720 us -> 0 us
  Pallas kernels: 0 us -> 336 us
  matrix products: 152 us -> 0 us
  local copies, waits for them, and re-layouts: 83.1 us -> 8.16 us
    reduce_scatter x2 -> x0, waiting for transfers between devices: 686 us -> none  [the longest x1 633 us: per_device(): lax.psum_scatter(partial_value, 'mp', scatter_dimension=2, tiled=True)]
    unnamed x8 -> x0, waiting for transfers between devices: 592 us -> none
    all_gather x3 -> x0, waiting for transfers between devices: 445 us -> none  [the longest x1 279 us: per_device(): lax.all_gather(cotangent, 'mp', axis=2, tiled=True)]
    pallas_call x0 -> x1, Pallas kernels: none -> 336 us  [run_layer(): pl.pallas_call(functools.partial(layer_kernel, n, d, clips, slot, sub), o...]
    dot_general x12 -> x0, matrix products: 152 us -> none  [the longest x1 27.2 us: per_device(): jnp.einsum('ckt,kj->cjt', hidden, out_low, preferred_element_type=jnp.flo...]
    add x2 -> x1, local copies, waits for them, and re-layouts: 50.1 us -> 0.01 us  [per_device(): inputs.astype(F32) + bro[:, 0].astype(F32) + bias_out[0][None, :, None]]
    slice x5 -> x2, local copies, waits for them, and re-layouts: 25 us -> 0.29 us  [the longest x1 0.22 us: per_device(): gw[:, taps]]
  transfers between devices with their start and end apart: 7 -> 0, of which waited for: 6 -> 0; matrix products, arithmetic and copies ran while one was open for 8% -> 0% of each run, Pallas kernels for 0% -> 0%
where the time goes in v1:
time: 374 us; the launch traced here: 370 us
  Pallas kernels  336 us (90%)
  other arithmetic  25.2 us (7%)
  local copies, waits for them, and re-layouts  8.16 us (2%)
    pallas_call x1, Pallas kernels, run_layer(): pl.pallas_call(functools.partial(layer_kernel, n, d, clips, slot, sub), o...  336 us

profile of v1, /device:TPU:0, one launch (start us, length us, event | category | flops | bytes accessed | tf_op | source)
XLA Modules:
  0.0 370.5 jit_solution(16544973301278342109)
XLA Ops:
  0.6 0.7 convert_element_type.54
  1.4 0.1 pad.27.clone
  1.4 0.1 pad.26.clone
  1.5 2.0 maximum_maximum_fusion.cnd
  3.5 1.0 convert_element_type.55
  4.5 1.1 convert_bitcast_fusion
  5.6 0.1 copy.34
  5.7 0.1 concatenate.13
  5.9 0.8 maximum_maximum_fusion.1.wcat
  6.7 2.9 convert_reduce_fusion
  9.6 0.1 copy.35
  9.7 0.6 pad.11.bsum
  10.3 336.2 %shard_map.244 = (bf16[2,2,64,8192]{3,2,1,0:T(8,128)(2,1)}, bf16[2,64,8192]{2,1,0:T(8,128)(2,1)}, bf16[2,64,1024]{2,1,0:T(8,128)(2,1)}, f32[2,128,1024]{2,1,0:T(8,128)}, f32[64,3584]{1,0:T(8,128)}) custom-call(bf16[2,64,8192]{2,1,0:T(8,128)(2,1)} %x.7, bf16[2,2,64,8192]{3,2,1,0:T(8,128)(2,1)} %cot.1, bf16[2,128,1024]{2,1,0:T(8,128)(2,1)} %maximum_maximum_fusion.cnd, ...), custom_call_target="tpu_custom_call" | custom-call | tf_op jit(solution)/shard_map/pallas_call | solution.py:269
  346.6 2.2 add_convert_fusion
  348.8 0.6 copy-done.1
  349.4 0.6 fusion.2
  350.0 2.4 pad_maximum_fusion
  352.5 0.1 slice.76
  352.6 2.5 pad_convert_fusion
  355.1 5.1 %reshape.52 = f32[2,64,8192]{2,1,0:T(8,128)} reshape(f32[2,64,8,1024]{3,2,1,0:T(8,128)} %pad_convert_fusion) | data formatting | bytes 8388608 | tf_op jit(solution)/shard_map/reshape | solution.py:358
  360.2 0.0 copy-start.2
  360.2 0.0 copy-start.6
  360.2 0.0 copy-start.7
  360.2 5.7 %convert_add_fusion = f32[2,64,8192]{2,1,0:T(8,128)} fusion(f32[2,64,8192]{2,1,0:T(8,128)} %reshape.52, bf16[2,64,8192]{2,1,0:T(8,128)(2,1)S(1)} %copy-done.3, bf16[2,2,64,8192]{3,2,1,0:T(8,128)(2,1)} %cot.1), kind=kLoop, calls=%fused_computation.2 | loop fusion | flops 4194304 | bytes 12582912 | tf_op jit(solution)/shard_map/add | solution.py:359
  365.9 0.0 copy-start.12
  365.9 0.0 copy-start.13
  365.9 0.0 copy-start.14
  366.0 0.9 slice_bitcast_fusion.1
  366.9 1.6 fusion.10
  368.6 1.1 fusion.8
  369.6 0.2 slice_reduce_fusion.3
  369.9 0.6 fusion.6
  (32 shorter events, 0.2 us)
Async XLA Ops:
  10.3 338.5 %copy-start = (bf16[2,64,8192]{2,1,0:T(8,128)(2,1)S(1)}, bf16[2,64,8192]{2,1,0:T(8,128)(2,1)}, u32[]{:S(2)}) copy-start(bf16[2,64,8192]{2,1,0:T(8,128)(2,1)} %x.7) | copy-start | bytes 6291460
  346.6 2.8 copy-start.1
  350.0 2.4 copy-start.11
  355.1 5.1 %copy-start.3 = (bf16[2,64,8192]{2,1,0:T(8,128)(2,1)S(1)}, bf16[2,64,8192]{2,1,0:T(8,128)(2,1)}, u32[]{:S(2)}) copy-start(bf16[2,64,8192]{2,1,0:T(8,128)(2,1)} %get-tuple-element.21) | copy-start | bytes 6291460
  360.2 5.7 %copy-start.8 = (f32[2,128,1024]{2,1,0:T(8,128)S(1)}, f32[2,128,1024]{2,1,0:T(8,128)}, u32[]{:S(2)}) copy-start(f32[2,128,1024]{2,1,0:T(8,128)} %get-tuple-element.23) | copy-start | bytes 3145732
  360.2 6.7 %copy-start.4 = (f32[64,3584]{1,0:T(8,128)S(1)}, f32[64,3584]{1,0:T(8,128)}, u32[]{:S(2)}) copy-start(f32[64,3584]{1,0:T(8,128)} %get-tuple-element.24) | copy-start | bytes 2752516
  360.2 6.7 %copy-start.2 = (f32[1104,2,64]{0,2,1:T(8,128)S(1)}, f32[1104,2,64]{0,2,1:T(8,128)}, u32[]{:S(2)}) copy-start(f32[1104,2,64]{0,2,1:T(8,128)} %param.17) | copy-start | bytes 1695748
  360.2 6.7 %copy-start.6 = (f32[1104,2,64]{0,2,1:T(8,128)S(1)}, f32[1104,2,64]{0,2,1:T(8,128)}, u32[]{:S(2)}) copy-start(f32[1104,2,64]{0,2,1:T(8,128)} %param.20) | copy-start | bytes 1695748
  360.2 6.7 %copy-start.7 = (f32[1104,2,64]{0,2,1:T(8,128)S(1)}, f32[1104,2,64]{0,2,1:T(8,128)}, u32[]{:S(2)}) copy-start(f32[1104,2,64]{0,2,1:T(8,128)} %param.23) | copy-start | bytes 1695748
  365.9 2.7 copy-start.5
  365.9 2.7 copy-start.9
  365.9 2.7 copy-start.10
  365.9 3.9 %copy-start.12 = (f32[4,64]{1,0:T(4,128)S(1)}, f32[4,64]{1,0:T(4,128)}, u32[]{:S(2)}) copy-start(f32[4,64]{1,0:T(4,128)} %param.19) | copy-start | bytes 3076
  365.9 3.9 %copy-start.13 = (f32[4,64]{1,0:T(4,128)S(1)}, f32[4,64]{1,0:T(4,128)}, u32[]{:S(2)}) copy-start(f32[4,64]{1,0:T(4,128)} %param.22) | copy-start | bytes 3076
  365.9 3.9 %copy-start.14 = (f32[4,64]{1,0:T(4,128)S(1)}, f32[4,64]{1,0:T(4,128)}, u32[]{:S(2)}) copy-start(f32[4,64]{1,0:T(4,128)} %param.25) | copy-start | bytes 3076

commit v2 on v1

v2 whole, which is shorter than its diff:
```python
import functools

import jax
import jax.numpy as jnp
from jax import lax
from jax.experimental import pallas as pl
from jax.experimental.pallas import tpu as pltpu
from jax.sharding import PartitionSpec as P

RESIDUAL_WIDTH = 512
GH = 512
DILATION_STEP = 32
STEP = 4

BETA_ONE = 0.5
BETA_TWO = 0.5
EPSILON = 1e-08
WEIGHT_DECAY = 0.01
CONV_RATE = 0.03
OUT_RATE = 0.1
BIAS_RATE = 0.3

MESH = pl.DeviceIdType.MESH
LANES = 128
HALF = RESIDUAL_WIDTH // 2
KP = 1152
OUT_AT = 2 * KP
USED = OUT_AT + 2 * HALF
WIDE = 3072
AHEAD = 10
OWN = 6
SLOTS = 4
BF = jnp.bfloat16
F32 = jnp.float32


def dot(a, b):
    return jnp.dot(a, b, preferred_element_type=F32)


def dot_nt(a, b):
    return lax.dot_general(a, b, (((1,), (1,)), ((), ())), preferred_element_type=F32)


def layer_kernel(
    n, d, clips, slot, sub, mel,
    x, cot, cond, lens, wcat, bsum,
    bro, gio, gco, gw, bs,
    xin, cin, cnd, grecv, gsend, gown, wall, wtr, pg, gacc, ost, gfs, gcs, r0, r1, s2,
    sem_fx, sem_fc, sem_send, sem_xh, sem_xm, sem_c, sem_k, sem_gm, sem_o, sem_gf, sem_gc, sem_in, sem_r1,
):
    g = lax.axis_index("dp")
    m = lax.axis_index("mp")
    r = RESIDUAL_WIDTH // n
    t = slot // n
    per = t // sub
    blocks = slot // sub
    piece = WIDE // d
    half = n // 2
    band = GH // clips
    share = n // clips
    h = m // half
    first = h * half
    local = m - first
    worker = jnp.logical_and(m >= half - clips, m < half + clips)
    wc = lax.rem(m + 2 * clips * n - (half - clips), clips)
    mirror = half - clips + (1 - h) * clips + wc
    group = m // share
    own_rows = jnp.logical_and(worker, group == wc)

    def wid(hh, c):
        return half - clips + hh * clips + c

    def lane(i, size=sub):
        return pl.ds(pl.multiple_of(i, LANES), size)

    def rows(j):
        return pl.ds(pl.multiple_of(j * r, r), r)

    def remote(src, dst, ss, rs, gg, j):
        return pltpu.make_async_remote_copy(
            src_ref=src, dst_ref=dst, send_sem=ss, recv_sem=rs,
            device_id=(gg, j), device_id_type=MESH,
        )

    def drain(ref, sem):
        pltpu.make_async_copy(ref, ref, sem).wait()

    bar = pltpu.get_barrier_semaphore()

    @pl.loop(1, n)
    def _(k):
        pl.semaphore_signal(bar, inc=1, device_id=(g, lax.rem(m + k, n)), device_id_type=MESH)

    @pl.loop(1, d)
    def _(k):
        pl.semaphore_signal(bar, inc=1, device_id=(lax.rem(g + k, d), m), device_id_type=MESH)

    pl.semaphore_wait(bar, n + d - 2)

    mine = lane(g * piece, piece)
    kept = pl.ds(pl.multiple_of(wc * band, band), band)

    def send_cond():
        for hh in range(2):
            for c in range(clips):
                to = wid(hh, c)
                dst = cnd.at[pl.ds(0, mel), lane(m * t, t)]

                @pl.when(to == m)
                def _():
                    pltpu.make_async_copy(cond.at[c], dst, sem_k.at[m]).start()

                @pl.when(to != m)
                def _():
                    remote(cond.at[c], dst, sem_send.at[0], sem_k.at[m], g, to).start()

    turn = jnp.maximum(m * per - 4, 0)

    for hh in range(2):
        to = wid(hh, group)

        @pl.when(to == m)
        def _():
            pltpu.make_async_copy(wcat.at[hh, :, mine], wall.at[rows(m), mine], sem_in.at[0]).start()

        @pl.when(to != m)
        def _():
            remote(wcat.at[hh, :, mine], wall.at[rows(m), mine], sem_send.at[1], sem_in.at[0], g, to).start()

    @pl.loop(1, d)
    def _(k):
        remote(bsum, bs.at[g], sem_send.at[2], sem_in.at[3], lax.rem(g + k, d), m).start()

    pltpu.make_async_copy(bsum, bs.at[g], sem_in.at[3]).start()

    def far():
        def send_x(s):
            at = s * sub

            @pl.when(s >= SLOTS)
            def _():
                drain(x.at[:, :, pl.ds(0, sub)], sem_fx.at[lax.rem(s, SLOTS)])

            for c in range(clips):
                remote(x.at[c, :, lane(at)], xin.at[rows(m), lane(at + LANES)],
                       sem_fx.at[lax.rem(s, SLOTS)], sem_xh.at[s], g, wid(h, c)).start()

        def send_cot(s):
            at = s * sub

            @pl.when(s >= SLOTS)
            def _():
                drain(cot.at[:, :, :, pl.ds(0, sub)], sem_fc.at[lax.rem(s, SLOTS)])

            for c in range(clips):
                remote(cot.at[c, :, :, lane(at)], cin.at[:, rows(local), lane(at)],
                       sem_fc.at[lax.rem(s, SLOTS)], sem_c.at[s], g, wid(h, c)).start()

        pl.loop(0, AHEAD)(send_x)

        @pl.loop(0, blocks)
        def _(s):
            @pl.when(s == turn)
            def _():
                send_cond()

            @pl.when(s + AHEAD < blocks)
            def _():
                send_x(s + AHEAD)

            send_cot(s)

        @pl.loop(0, SLOTS)
        def _(q):
            drain(x.at[:, :, pl.ds(0, sub)], sem_fx.at[q])
            drain(cot.at[:, :, :, pl.ds(0, sub)], sem_fc.at[q])

    def work():
        def own(s):
            at = s * sub
            for k in range(1, clips):
                c = lax.rem(wc + k, clips)
                remote(x.at[c, :, lane(at)], xin.at[rows(m), lane(at + LANES)],
                       sem_send.at[3], sem_xh.at[s], g, wid(h, c)).start()
                remote(cot.at[c, :, :, lane(at)], cin.at[:, rows(local), lane(at)],
                       sem_send.at[4], sem_c.at[s], g, wid(h, c)).start()
            pltpu.make_async_copy(x.at[wc, :, lane(at)], xin.at[rows(m), lane(at + LANES)], sem_xh.at[s]).start()
            pltpu.make_async_copy(cot.at[wc, :, :, lane(at)], cin.at[:, rows(local), lane(at)], sem_c.at[s]).start()

        here = pl.ds(pl.multiple_of(h * HALF, HALF), HALF)
        there = pl.ds(pl.multiple_of((1 - h) * HALF, HALF), HALF)

        def relay(s):
            part = xin.at[here, lane(s * sub + LANES)]
            drain(part, sem_xh.at[s])
            remote(part, part, sem_send.at[5], sem_xm.at[s], g, mirror).start()

        pl.loop(0, OWN)(own)

        xin[:, 0:LANES] = jnp.zeros((RESIDUAL_WIDTH, LANES), BF)
        pg[...] = jnp.zeros_like(pg)
        cnd[mel:LANES, :] = (
            lax.broadcasted_iota(jnp.int32, (LANES - mel, slot), 0) == 0
        ).astype(F32).astype(BF)
        gacc[...] = jnp.zeros_like(gacc)

        pl.loop(0, 3)(relay)
        drain(wall.at[kept, mine], sem_in.at[0])

        @pl.loop(1, d)
        def _(k):
            remote(wall.at[kept, mine], wall.at[kept, mine], sem_send.at[6], sem_in.at[1],
                   lax.rem(g + k, d), m).start()

        pl.loop(3, OWN)(relay)
        drain(wall.at[kept, pl.ds(0, (d - 1) * piece)], sem_in.at[1])
        for k in range(1, clips):
            remote(wall.at[kept, :], wall.at[kept, :], sem_send.at[7], sem_in.at[2], g,
                   wid(h, lax.rem(wc + k, clips))).start()
        pl.loop(OWN, AHEAD)(lambda s: (own(s), relay(s))[0])
        pl.loop(AHEAD, AHEAD + OWN)(own)
        drain(wall.at[pl.ds(0, GH - band), :], sem_in.at[2])

        @pl.loop(0, USED // LANES)
        def _(i):
            wtr[pl.ds(pl.multiple_of(i * LANES, LANES), LANES), :] = wall[:, lane(i * LANES, LANES)].T

        length = lens[wc]

        def back(top):
            win = pg[...]
            pn = win[:, :sub]
            pe = pltpu.roll(win, sub + LANES - DILATION_STEP, 1)[:, :sub]

            def tap(base):
                return wtr[pl.ds(pl.multiple_of(base + top, HALF), HALF), :]

            return (dot(tap(512), pn[0:512]) + dot(wtr[pl.ds(pl.multiple_of(KP + 512 + top, LANES), HALF), :], pn[512:1024])
                    + dot(tap(0), pe[0:512]) + dot(wtr[pl.ds(pl.multiple_of(KP + top, LANES), HALF), :], pe[512:1024]))

        def give(q):
            remote(gsend.at[:, lane((q + 1) * sub)], grecv.at[:, lane(q * sub)],
                   sem_send.at[8], sem_gm.at[q], g, mirror).start()

        def combine(q):
            now = lane(q * sub)
            z = lax.rem(q, SLOTS)
            drain(grecv.at[:, now], sem_gm.at[q])

            @pl.when(q >= SLOTS)
            def _():
                drain(gfs.at[z], sem_gf.at[z])

            gfs[z] = (gown[:, lane((q + 1) * sub)].astype(F32) + grecv[:, now].astype(F32)).astype(BF)

            @pl.loop(1, half)
            def _(k):
                i = lax.rem(local + k, half)
                remote(gfs.at[z, rows(i), :], gio.at[wc, :, now], sem_gf.at[z], sem_in.at[5], g, first + i).start()

            pltpu.make_async_copy(gfs.at[z, rows(local), :], gio.at[wc, :, now], sem_gf.at[z]).start()

        @pl.loop(0, blocks)
        def _(s):
            at = s * sub
            now = lane(at)
            off = lane(at + LANES)
            z = lax.rem(s, SLOTS)

            @pl.when(s == turn)
            def _():
                send_cond()

            @pl.when(s + AHEAD + OWN < blocks)
            def _():
                own(s + AHEAD + OWN)

            @pl.when(s + AHEAD < blocks)
            def _():
                relay(s + AHEAD)

            @pl.when(lax.rem(s, per) == 0)
            def _():
                drain(cnd.at[pl.ds(0, mel), lane((s // per) * t, t)], sem_k.at[s // per])

            drain(xin.at[there, off], sem_xm.at[s])
            drain(cin.at[:, :, now], sem_c.at[s])

            xc = xin[:, off]
            xe = pltpu.roll(xin[:, lane(at, sub + LANES)], DILATION_STEP, 1)[:, LANES:]
            cd = cnd[:, now]
            pre_f = (dot(wall[:, 0:512], xe) + dot(wall[:, 512:1024], xc) + dot(wall[:, 1024:KP], cd))
            pre_g = (dot(wall[:, KP:KP + 512], xe) + dot(wall[:, KP + 512:KP + 1024], xc)
                     + dot(wall[:, KP + 1024:OUT_AT], cd))
            place = at + lax.broadcasted_iota(jnp.int32, (1, sub), 1)
            keep = (place < length).astype(F32)
            th = jnp.tanh(pre_f)
            sg = jax.nn.sigmoid(pre_g)
            hid = (keep * th * sg).astype(BF)
            branch = dot(wtr[OUT_AT:USED, :], hid).astype(BF)

            @pl.when(s >= SLOTS)
            def _():
                drain(ost.at[z], sem_o.at[z])
                drain(gcs.at[z], sem_gc.at[z])

            ost[z, 0] = branch[0:HALF]
            ost[z, 1] = branch[HALF:]

            @pl.loop(1, half)
            def _(k):
                i = lax.rem(local + k, half)
                remote(ost.at[z, :, rows(i), :], bro.at[wc, :, :, now], sem_o.at[z], sem_in.at[4], g, first + i).start()

            pltpu.make_async_copy(ost.at[z, :, rows(local), :], bro.at[wc, :, :, now], sem_o.at[z]).start()

            ct = cin[:, :, now].reshape(2 * HALF, sub)
            hg = dot(wall[:, OUT_AT:USED], ct) * keep
            pgf = (hg * sg * (1.0 - th * th)).astype(BF)
            pgg = (hg * th * sg * (1.0 - sg)).astype(BF)
            pg[0:512, sub:] = pgf[:, :LANES]
            pg[512:1024, sub:] = pgg[:, :LANES]
            gacc[:, 0:512] += dot_nt(pgf, xe)
            gacc[:, 512:1024] += dot_nt(pgf, xc)
            gacc[:, 1024:KP] += dot_nt(pgf, cd)
            gacc[:, KP:KP + 512] += dot_nt(pgg, xe)
            gacc[:, KP + 512:KP + 1024] += dot_nt(pgg, xc)
            gacc[:, KP + 1024:OUT_AT] += dot_nt(pgg, cd)
            gacc[:, OUT_AT:USED] += dot_nt(hid, ct)
            gcs[z] = (dot(wtr[1024:KP, :], pgf) + dot(wtr[KP + 1024:OUT_AT, :], pgg))[0:mel].astype(BF)
            keeper = s // per
            spot = gco.at[h * clips + wc, :, lane(at - keeper * t)]

            @pl.when(keeper == m)
            def _():
                pltpu.make_async_copy(gcs.at[z], spot, sem_gc.at[z]).start()

            @pl.when(keeper != m)
            def _():
                remote(gcs.at[z], spot, sem_gc.at[z], sem_in.at[6], g, keeper).start()

            gsend[:, now] = back((1 - h) * HALF).astype(BF)
            gown[:, now] = back(h * HALF).astype(BF)
            pg[0:512, 0:sub] = pgf
            pg[512:1024, 0:sub] = pgg

            @pl.when(lax.rem(s, 2) == 0)
            def _():
                @pl.when(s >= 2)
                def _():
                    give(s // 2 - 1)

                @pl.when(s >= 10)
                def _():
                    combine(s // 2 - 5)

        pg[:, sub:] = jnp.zeros((2 * GH, LANES), BF)
        gsend[:, pl.ds(slot, sub)] = back((1 - h) * HALF).astype(BF)
        gown[:, pl.ds(slot, sub)] = back(h * HALF).astype(BF)

        s0 = cin.at[0, :, pl.ds(0, WIDE)]
        for k in range(1, clips):
            to = lax.rem(wc + k, clips)
            s0[...] = gacc[pl.ds(pl.multiple_of(to * band, band), band), :].astype(BF)
            remote(s0, r0.at[k - 1], sem_send.at[9], sem_in.at[7], g, wid(h, to)).start()

        pl.loop(blocks // 2 - 1, blocks)(give)
        mid = blocks // 2 - 5
        step = (blocks - mid) // 4
        pl.loop(mid, mid + step)(combine)
        drain(r0, sem_in.at[7])
        for k in range(1, clips):
            gacc[kept, :] += r0[k - 1].astype(F32)

        @pl.loop(1, d)
        def _(k):
            to = lax.rem(g + k, d)
            src = cin.at[1, :, lane((k - 1) * piece, piece)]
            src[...] = gacc[kept, lane(to * piece, piece)].astype(BF)
            remote(src, r1.at[k - 1], sem_send.at[10], sem_r1.at[k - 1], to, m).start()

        pl.loop(mid + step, mid + 2 * step)(combine)

        @pl.loop(1, d)
        def _(k):
            drain(r1.at[k - 1], sem_r1.at[k - 1])
            gacc[kept, mine] += r1[k - 1].astype(F32)

        s2[...] = gacc[kept, mine].astype(BF)

        @pl.loop(0, share)
        def _(k):
            j = wc * share + k

            @pl.when(j == m)
            def _():
                pltpu.make_async_copy(s2.at[rows(k), :], gw.at[h, :, mine], sem_in.at[8]).start()

            @pl.when(j != m)
            def _():
                remote(s2.at[rows(k), :], gw.at[h, :, mine], sem_send.at[11], sem_in.at[8], g, j).start()

        pl.loop(mid + 2 * step, mid + 3 * step)(combine)
        share_out()
        pl.loop(mid + 3 * step, blocks)(combine)

        @pl.loop(0, SLOTS)
        def _(q):
            drain(ost.at[q], sem_o.at[q])
            drain(gcs.at[q], sem_gc.at[q])
            drain(gfs.at[q], sem_gf.at[q])

        drain(x.at[pl.ds(0, clips - 1)], sem_send.at[3])
        drain(cot.at[pl.ds(0, clips - 1)], sem_send.at[4])
        drain(xin.at[pl.ds(0, HALF), pl.ds(0, slot)], sem_send.at[5])
        drain(wall.at[kept, pl.ds(0, (d - 1) * piece)], sem_send.at[6])
        drain(wall.at[pl.ds(0, GH - band), :], sem_send.at[7])
        drain(gsend.at[:, pl.ds(0, slot)], sem_send.at[8])
        drain(r0, sem_send.at[9])
        drain(r1, sem_send.at[10])

    def share_out():
        drain(gw.at[:, :, mine], sem_in.at[8])

        @pl.loop(1, d)
        def _(k):
            remote(gw.at[:, :, mine], gw.at[:, :, mine], sem_send.at[12], sem_in.at[9], lax.rem(g + k, d), m).start()

    @pl.when(worker)
    def _():
        work()
        drain(gco.at[pl.ds(0, 2 * clips - 1)], sem_send.at[0])
        drain(bro.at[pl.ds(0, clips - 1)], sem_in.at[4])
        drain(gio.at[pl.ds(0, clips - 1)], sem_in.at[5])
        drain(gco.at[pl.ds(0, 2 * clips - 1)], sem_in.at[6])

        @pl.when(own_rows)
        def _():
            drain(wcat.at[0, :, mine], sem_send.at[1])
            drain(s2.at[pl.ds(0, (share - 1) * r), :], sem_send.at[11])

        @pl.when(jnp.logical_not(own_rows))
        def _():
            drain(wcat.at[:, :, mine], sem_send.at[1])
            drain(s2, sem_send.at[11])

    @pl.when(jnp.logical_not(worker))
    def _():
        far()
        share_out()
        drain(gco, sem_send.at[0])
        drain(wcat.at[:, :, mine], sem_send.at[1])
        drain(bro, sem_in.at[4])
        drain(gio, sem_in.at[5])
        drain(gco, sem_in.at[6])

    drain(gw.at[:, :, pl.ds(0, (d - 1) * piece)], sem_in.at[9])
    drain(gw.at[:, :, pl.ds(0, (d - 1) * piece)], sem_send.at[12])
    drain(bs, sem_in.at[3])
    drain(bs.at[pl.ds(0, d - 1)], sem_send.at[2])


def run_layer(n, d, x, cot, cond, lens, wcat, bsum):
    clips, r, slot = x.shape
    mel = cond.shape[1]
    t = slot // n
    sub = min(256, t)
    blocks = slot // sub
    piece = WIDE // d
    width = RESIDUAL_WIDTH
    band = GH // clips
    any_spec = pl.BlockSpec(memory_space=pl.ANY)
    vmem = pl.BlockSpec(memory_space=pltpu.VMEM)
    smem = pl.BlockSpec(memory_space=pltpu.SMEM)
    dma = pltpu.SemaphoreType.DMA
    return pl.pallas_call(
        functools.partial(layer_kernel, n, d, clips, slot, sub, mel),
        out_shape=(
            jax.ShapeDtypeStruct((clips, 2, r, slot), BF),
            jax.ShapeDtypeStruct((clips, r, slot), BF),
            jax.ShapeDtypeStruct((2 * clips, mel, t), BF),
            jax.ShapeDtypeStruct((2, r, WIDE), BF),
            jax.ShapeDtypeStruct((d, r, LANES), F32),
        ),
        in_specs=[any_spec, any_spec, any_spec, smem, vmem, vmem],
        out_specs=(any_spec, any_spec, any_spec, vmem, vmem),
        scratch_shapes=[
            pltpu.VMEM((width, LANES + slot), BF),
            pltpu.VMEM((2, HALF, slot), BF),
            pltpu.VMEM((LANES, slot), BF),
            pltpu.VMEM((HALF, slot), BF),
            pltpu.VMEM((HALF, slot + sub), BF),
            pltpu.VMEM((HALF, slot + sub), BF),
            pltpu.VMEM((GH, WIDE), BF),
            pltpu.VMEM((USED, GH), BF),
            pltpu.VMEM((2 * GH, sub + LANES), BF),
            pltpu.VMEM((GH, WIDE), F32),
            pltpu.VMEM((SLOTS, 2, HALF, sub), BF),
            pltpu.VMEM((SLOTS, HALF, sub), BF),
            pltpu.VMEM((SLOTS, mel, sub), BF),
            pltpu.VMEM((clips - 1, band, WIDE), BF),
            pltpu.VMEM((d - 1, band, piece), BF),
            pltpu.VMEM((band, piece), BF),
            dma((SLOTS,)),
            dma((SLOTS,)),
            dma((13,)),
            dma((blocks,)),
            dma((blocks,)),
            dma((blocks,)),
            dma((n,)),
            dma((blocks,)),
            dma((SLOTS,)),
            dma((SLOTS,)),
            dma((SLOTS,)),
            dma((10,)),
            dma((d - 1,)),
        ],
        compiler_params=pltpu.CompilerParams(
            collective_id=0, has_side_effects=True, vmem_limit_bytes=60 << 20
        ),
    )(x, cot, cond, lens, wcat, bsum)


def adamw(master, first_old, second_old, gradient, step_rate, power_one, power_two):
    first_new = BETA_ONE * first_old + (1.0 - BETA_ONE) * gradient
    second_new = BETA_TWO * second_old + (1.0 - BETA_TWO) * gradient * gradient
    first_hat = first_new / (1.0 - power_one)
    second_hat = second_new / (1.0 - power_two)
    renewed = master - step_rate * (
        first_hat / (jnp.sqrt(second_hat) + EPSILON) + WEIGHT_DECAY * master
    )
    return (renewed, first_new, second_new)


def per_device(
    n, d,
    inputs, conditioning, lengths, cotangent, conv_weight, out_weight, biases,
    conv_first, out_first, bias_first, conv_second, out_second, bias_second,
):
    clips, r, slot = inputs.shape
    taps = conv_weight.shape[0]
    bias_low = biases.astype(BF)
    flipped = jnp.transpose(conv_weight.astype(BF), (1, 2, 0))
    flipped = jnp.concatenate(
        [flipped, bias_low[0:2, :, None], jnp.zeros((2, r, KP - taps - 1), BF)], axis=2
    )
    out_low = out_weight.astype(BF).reshape(r, 2, 2, HALF)
    wcat = jnp.stack(
        [
            jnp.concatenate(
                [
                    flipped[0],
                    flipped[1],
                    out_low[:, 0, side],
                    out_low[:, 1, side],
                    jnp.zeros((r, WIDE - USED), BF),
                ],
                axis=1,
            )
            for side in range(2)
        ],
        axis=0,
    )
    cond = jnp.transpose(conditioning, (0, 2, 1))
    sums = jnp.sum(cotangent.astype(F32), axis=(0, 3))
    bsum = jnp.pad(sums.T, ((0, 0), (0, LANES - 2)))
    bro, gio, gco, gw, bs = run_layer(n, d, inputs, cotangent, cond, lengths, wcat, bsum)

    bias_out = bias_low[2:4].astype(F32)
    layer_out = jnp.stack(
        [
            inputs.astype(F32) + bro[:, 0].astype(F32) + bias_out[0][None, :, None],
            bro[:, 1].astype(F32) + bias_out[1][None, :, None],
        ],
        axis=1,
    ).astype(BF)
    grad_input = cotangent[:, 0].astype(F32) + gio.astype(F32)
    grad_cond = jnp.transpose(gco[:clips].astype(F32) + gco[clips:].astype(F32), (0, 2, 1))
    gsum = gw[0, :, :OUT_AT].astype(F32) + gw[1, :, :OUT_AT].astype(F32)
    conv_grad = jnp.transpose(
        jnp.stack([gsum[:, :taps], gsum[:, KP : KP + taps]], axis=0), (2, 0, 1)
    )
    out_grad = jnp.stack(
        [gw[:, :, OUT_AT : OUT_AT + HALF], gw[:, :, OUT_AT + HALF : USED]], axis=0
    )
    out_grad = jnp.transpose(out_grad, (2, 0, 1, 3)).reshape(r, 4 * HALF).astype(F32)
    bsums = jnp.sum(bs, axis=0)
    bias_grad = jnp.stack([gsum[:, taps], gsum[:, KP + taps], bsums[:, 0], bsums[:, 1]], axis=0)
    power_one = jnp.float32(BETA_ONE**STEP)
    power_two = jnp.float32(BETA_TWO**STEP)
    conv_new = adamw(
        conv_weight, conv_first, conv_second, conv_grad, CONV_RATE, power_one, power_two
    )
    out_new = adamw(out_weight, out_first, out_second, out_grad, OUT_RATE, power_one, power_two)
    bias_new = adamw(biases, bias_first, bias_second, bias_grad, BIAS_RATE, power_one, power_two)
    return (
        layer_out,
        grad_input,
        grad_cond,
        conv_new[0],
        out_new[0],
        bias_new[0],
        conv_new[1],
        out_new[1],
        bias_new[1],
        conv_new[2],
        out_new[2],
        bias_new[2],
        conv_new[0].astype(BF),
        out_new[0].astype(BF),
        bias_new[0].astype(BF),
    )


def solution(mesh):
    in_specs = (
        P("dp", "mp", None),
        P("dp", "mp", None),
        P("dp"),
        P("dp", None, "mp", None),
        P(None, None, "mp"),
        P("mp", None),
        P(None, "mp"),
        P(None, None, "mp"),
        P("mp", None),
        P(None, "mp"),
        P(None, None, "mp"),
        P("mp", None),
        P(None, "mp"),
    )
    out_specs = (
        P("dp", None, "mp", None),
        P("dp", "mp", None),
        P("dp", "mp", None),
        P(None, None, "mp"),
        P("mp", None),
        P(None, "mp"),
        P(None, None, "mp"),
        P("mp", None),
        P(None, "mp"),
        P(None, None, "mp"),
        P("mp", None),
        P(None, "mp"),
        P(None, None, "mp"),
        P("mp", None),
        P(None, "mp"),
    )
    return jax.shard_map(
        functools.partial(per_device, mesh.shape["mp"], mesh.shape["dp"]),
        mesh=mesh, in_specs=in_specs, out_specs=out_specs, check_vma=False,
    )
```

time: 374 us -> 275 us (0.74)
  Pallas kernels: 336 us -> 249 us
  other arithmetic: 25.2 us -> 18.8 us
    pallas_call x1, Pallas kernels: 336 us -> 249 us  [run_layer(): pl.pallas_call(functools.partial(layer_kernel, n, d, clips, slot, sub, me...]
    reshape x1, local copies, waits for them, and re-layouts: 5.09 us -> 0.08 us  [per_device(): out_low = out_weight.astype(BF).reshape(r, 2, 2, HALF)]
where the time goes in v2:
time: 275 us; the launch traced here: 274 us
  Pallas kernels  249 us (91%)
  other arithmetic  18.8 us (7%)
  local copies, waits for them, and re-layouts  4.67 us (2%)
    pallas_call x1, Pallas kernels, run_layer(): pl.pallas_call(functools.partial(layer_kernel, n, d, clips, slot, sub, me...  249 us

profile of v2, /device:TPU:0, one launch (start us, length us, event | category | flops | bytes accessed | tf_op | source)
XLA Modules:
  0.0 273.7 jit_solution(16638640709855125625)
XLA Ops:
  0.6 0.7 convert_element_type.74
  1.3 1.1 convert_bitcast_fusion
  2.4 0.1 copy.48
  2.6 0.1 concatenate.9
  2.8 1.0 convert_element_type.75
  3.8 0.1 reshape.45
  3.8 0.2 fusion.20
  4.1 0.9 pad_maximum_fusion.1.wcat
  5.0 2.9 %convert_reduce_fusion = f32[2,64]{1,0:T(2,128)S(1)} fusion(bf16[2,2,64,8192]{3,2,1,0:T(8,128)(2,1)} %cot.1), kind=kLoop, calls=%fused_computation | loop fusion | flops 4194176 | bytes 4194816 | tf_op jit(solution)/shard_map/reduce_sum | solution.py:566
  7.9 0.1 copy.53
  8.0 0.6 pad.4.bsum
  8.7 249.3 %shard_map.244 = (bf16[2,2,64,8192]{3,2,1,0:T(8,128)(2,1)}, bf16[2,64,8192]{2,1,0:T(8,128)(2,1)}, bf16[4,80,1024]{2,1,0:T(8,128)(2,1)}, bf16[2,64,3072]{2,1,0:T(8,128)(2,1)}, f32[4,64,128]{2,1,0:T(8,128)}) custom-call(bf16[2,64,8192]{2,1,0:T(8,128)(2,1)} %x.3, bf16[2,2,64,8192]{3,2,1,0:T(8,128)(2,1)} %cot.1, bf16[2,80,1024]{2,1,0:T(8,128)(2,1)} %bitcast.80, ...), custom_call_target="tpu_custom_call" | custom-call | tf_op jit(solution)/shard_map/pallas_call | solution.py:477
  258.0 2.2 add_convert_fusion
  260.2 0.6 copy-done.2
  260.8 0.6 fusion.2
  261.5 0.0 copy-start
  261.5 2.5 pad_maximum_fusion
  264.0 1.2 copy-done
  265.2 0.7 copy-done.4
  265.9 0.0 copy-start.9
  265.9 2.5 convert_add_fusion
  268.4 0.9 add_bitcast_fusion
  269.3 0.1 add_bitcast_fusion.1
  269.5 0.0 copy-start.13
  269.5 0.0 copy-start.14
  269.5 1.6 fusion.18
  271.2 0.2 copy.56
  271.4 0.2 reshape.48
  271.7 1.0 fusion.16
  272.7 0.2 slice_reduce_fusion.1
  272.9 0.2 slice_reduce_fusion.3
  273.1 0.6 fusion.14
  (40 shorter events, 0.2 us)
Async XLA Ops:
  8.7 251.6 %copy-start.1 = (bf16[2,64,8192]{2,1,0:T(8,128)(2,1)S(1)}, bf16[2,64,8192]{2,1,0:T(8,128)(2,1)}, u32[]{:S(2)}) copy-start(bf16[2,64,8192]{2,1,0:T(8,128)(2,1)} %x.3) | copy-start | bytes 6291460
  258.0 2.8 %copy-start.2 = (bf16[2,2,64,8192]{3,2,1,0:T(8,128)(2,1)S(1)}, bf16[2,2,64,8192]{3,2,1,0:T(8,128)(2,1)}, u32[]{:S(2)}) copy-start(bf16[2,2,64,8192]{3,2,1,0:T(8,128)(2,1)} %get-tuple-element.20) | copy-start | bytes 12582916
  261.5 3.7 %copy-start = (bf16[2,2,64,8192]{3,2,1,0:T(8,128)(2,1)S(1)}, bf16[2,2,64,8192]{3,2,1,0:T(8,128)(2,1)}, u32[]{:S(2)}) copy-start(bf16[2,2,64,8192]{3,2,1,0:T(8,128)(2,1)} %cot.1) | copy-start | bytes 12582916
  261.5 4.4 %copy-start.4 = (bf16[2,64,8192]{2,1,0:T(8,128)(2,1)S(1)}, bf16[2,64,8192]{2,1,0:T(8,128)(2,1)}, u32[]{:S(2)}) copy-start(bf16[2,64,8192]{2,1,0:T(8,128)(2,1)} %get-tuple-element.21) | copy-start | bytes 6291460
  265.9 2.6 copy-start.7
  265.9 3.5 %copy-start.6 = (bf16[2,64,3072]{2,1,0:T(8,128)(2,1)S(1)}, bf16[2,64,3072]{2,1,0:T(8,128)(2,1)}, u32[]{:S(2)}) copy-start(bf16[2,64,3072]{2,1,0:T(8,128)(2,1)} %get-tuple-element.23) | copy-start | bytes 2359300
  265.9 3.6 %copy-start.3 = (f32[1104,2,64]{0,2,1:T(8,128)S(1)}, f32[1104,2,64]{0,2,1:T(8,128)}, u32[]{:S(2)}) copy-start(f32[1104,2,64]{0,2,1:T(8,128)} %param.17) | copy-start | bytes 1695748
  265.9 3.6 %copy-start.8 = (f32[1104,2,64]{0,2,1:T(8,128)S(1)}, f32[1104,2,64]{0,2,1:T(8,128)}, u32[]{:S(2)}) copy-start(f32[1104,2,64]{0,2,1:T(8,128)} %param.20) | copy-start | bytes 1695748
  265.9 3.6 %copy-start.9 = (f32[1104,2,64]{0,2,1:T(8,128)S(1)}, f32[1104,2,64]{0,2,1:T(8,128)}, u32[]{:S(2)}) copy-start(f32[1104,2,64]{0,2,1:T(8,128)} %param.23) | copy-start | bytes 1695748
  269.3 2.3 copy-start.5
  269.3 2.3 copy-start.10
  269.3 2.3 copy-start.11
  269.5 3.3 %copy-start.12 = (f32[4,64,128]{2,1,0:T(8,128)S(1)}, f32[4,64,128]{2,1,0:T(8,128)}, u32[]{:S(2)}) copy-start(f32[4,64,128]{2,1,0:T(8,128)} %get-tuple-element.24) | copy-start | bytes 393220
  269.5 3.6 %copy-start.13 = (f32[4,64]{1,0:T(4,128)S(1)}, f32[4,64]{1,0:T(4,128)}, u32[]{:S(2)}) copy-start(f32[4,64]{1,0:T(4,128)} %param.19) | copy-start | bytes 3076
  269.5 3.6 %copy-start.14 = (f32[4,64]{1,0:T(4,128)S(1)}, f32[4,64]{1,0:T(4,128)}, u32[]{:S(2)}) copy-start(f32[4,64]{1,0:T(4,128)} %param.22) | copy-start | bytes 3076
  269.5 3.6 %copy-start.15 = (f32[4,64]{1,0:T(4,128)S(1)}, f32[4,64]{1,0:T(4,128)}, u32[]{:S(2)}) copy-start(f32[4,64]{1,0:T(4,128)} %param.25) | copy-start | bytes 3076

commit v3 on v2

v3 whole, which is shorter than its diff:
```python
import functools

import jax
import jax.numpy as jnp
from jax import lax
from jax.experimental import pallas as pl
from jax.experimental.pallas import tpu as pltpu
from jax.sharding import PartitionSpec as P

RESIDUAL_WIDTH = 512
GH = 512
DILATION_STEP = 32
STEP = 4

BETA_ONE = 0.5
BETA_TWO = 0.5
EPSILON = 1e-08
WEIGHT_DECAY = 0.01
CONV_RATE = 0.03
OUT_RATE = 0.1
BIAS_RATE = 0.3

MESH = pl.DeviceIdType.MESH
LANES = 128
HALF = RESIDUAL_WIDTH // 2
KP = 1152
OUT_AT = 2 * KP
USED = OUT_AT + 2 * HALF
WIDE = 3072
AHEAD = 16
OWN = 6
DIRECT = 6
GIVE = 14
LAG = 8
SLOTS = 4
LATE = 12
POSTS = 8
BF = jnp.bfloat16
F32 = jnp.float32


def dot(a, b):
    return jnp.dot(a, b, preferred_element_type=F32)


def dot_nt(a, b):
    return lax.dot_general(a, b, (((1,), (1,)), ((), ())), preferred_element_type=F32)


def layer_kernel(
    n, d, clips, slot, sub, mel,
    x, cot, cond, lens, wcat,
    bro, gio, gco, gw,
    xin, cin, cnd, grecv, gsend, gown, wall, wfw, wtr, pg, gacc, csum, ost, gfs, gk, kr, r0, r1, s2, r2,
    sem_fx, sem_fc, sem_send, sem_xh, sem_xm, sem_c, sem_k, sem_km, sem_kr, sem_gm, sem_gv, sem_o, sem_gf, sem_in, sem_r1,
):
    g = lax.axis_index("dp")
    m = lax.axis_index("mp")
    r = RESIDUAL_WIDTH // n
    t = slot // n
    per = t // sub
    blocks = slot // sub
    piece = WIDE // d
    half = n // 2
    band = GH // clips
    h = m // half
    first = h * half
    local = m - first
    worker = jnp.logical_and(m >= half - clips, m < half + clips)
    wc = lax.rem(m + 2 * clips * n - (half - clips), clips)
    mirror = half - clips + (1 - h) * clips + wc
    hub = jnp.logical_and(worker, wc == h)
    shared = (g + 1) * piece <= OUT_AT

    def wid(hh, c):
        return half - clips + hh * clips + c

    def lane(i, size=sub):
        return pl.ds(pl.multiple_of(i, LANES), size)

    def rows(j):
        return pl.ds(pl.multiple_of(j * r, r), r)

    def remote(src, dst, ss, rs, gg, j):
        return pltpu.make_async_remote_copy(
            src_ref=src, dst_ref=dst, send_sem=ss, recv_sem=rs,
            device_id=(gg, j), device_id_type=MESH,
        )

    def others(body):
        if half <= 4:
            for k in range(1, half):
                body(lax.rem(local + k, half))
        else:
            pl.loop(1, half)(lambda k: body(lax.rem(local + k, half)))

    def drain(ref, sem):
        pltpu.make_async_copy(ref, ref, sem).wait()

    def whole(ref, count, sem):
        drain(ref.at[0, :, pl.ds(0, count * piece)] if count <= d else ref.at[:, :, pl.ds(0, count // 2 * piece)], sem)

    bar = pltpu.get_barrier_semaphore()

    @pl.loop(1, half)
    def _(k):
        pl.semaphore_signal(bar, inc=1, device_id=(g, first + lax.rem(local + k, half)), device_id_type=MESH)

    @pl.loop(1, d)
    def _(k):
        pl.semaphore_signal(bar, inc=1, device_id=(lax.rem(g + k, d), m), device_id_type=MESH)

    @pl.when(worker)
    def _():
        for c in range(clips):
            pl.semaphore_signal(bar, inc=1, device_id=(g, wid(1 - h, c)), device_id_type=MESH)
        pl.semaphore_wait(bar, half + d - 2 + clips)

    @pl.when(jnp.logical_not(worker))
    def _():
        pl.semaphore_wait(bar, half + d - 2)

    mine = lane(g * piece, piece)
    kept = pl.ds(pl.multiple_of(wc * band, band), band)

    def send_cond(s):
        @pl.when(s // per == m)
        def _():
            dst = cnd.at[pl.ds(0, mel), lane(s * sub)]
            for c in range(clips):
                to = wid(h, c)
                part = cond.at[c, :, lane(s * sub - m * t)]

                @pl.when(to == m)
                def _():
                    pltpu.make_async_copy(part, dst, sem_k.at[s]).start()

                @pl.when(to != m)
                def _():
                    remote(part, dst, sem_send.at[0], sem_k.at[s], g, to).start()

    def in_half(s):
        return s // (blocks // 2) == h

    def weights():
        @pl.when(hub)
        def _():
            pltpu.make_async_copy(wcat.at[h, :, mine], wall.at[rows(m), mine], sem_in.at[0]).start()
            pltpu.make_async_copy(wcat.at[1 - h, :, mine], wfw.at[rows(local), :], sem_in.at[3]).start()

        @pl.when(jnp.logical_not(hub))
        def _():
            remote(wcat.at[h, :, mine], wall.at[rows(m), mine], sem_send.at[1], sem_in.at[0], g, wid(h, h)).start()
            remote(wcat.at[1 - h, :, mine], wfw.at[rows(local), :], sem_send.at[1], sem_in.at[3], g, wid(h, h)).start()

    def far():
        def send_x(s):
            at = s * sub

            @pl.when(s >= SLOTS)
            def _():
                drain(x.at[:, :, pl.ds(0, sub)], sem_fx.at[lax.rem(s, SLOTS)])

            for c in range(clips):
                remote(x.at[c, :, lane(at)], xin.at[rows(m), lane(at + LANES)],
                       sem_fx.at[lax.rem(s, SLOTS)], sem_xh.at[s], g, wid(h, c)).start()
            send_cond(s)

        def send_cot(s):
            at = s * sub

            @pl.when(s >= SLOTS)
            def _():
                drain(cot.at[:, :, :, pl.ds(0, sub)], sem_fc.at[lax.rem(s, SLOTS)])

            for c in range(clips):
                remote(cot.at[c, :, :, lane(at)], cin.at[:, rows(local), lane(at)],
                       sem_fc.at[lax.rem(s, SLOTS)], sem_c.at[s], g, wid(h, c)).start()

        pl.loop(0, 2)(send_x)
        weights()
        pl.loop(2, AHEAD)(send_x)

        @pl.loop(0, blocks)
        def _(s):
            @pl.when(s + AHEAD < blocks)
            def _():
                send_x(s + AHEAD)

            send_cot(s)

        @pl.loop(0, SLOTS)
        def _(q):
            drain(x.at[:, :, pl.ds(0, sub)], sem_fx.at[q])
            drain(cot.at[:, :, :, pl.ds(0, sub)], sem_fc.at[q])

    def work():
        def own(s):
            at = s * sub
            for k in range(1, clips):
                c = lax.rem(wc + k, clips)
                remote(x.at[c, :, lane(at)], xin.at[rows(m), lane(at + LANES)],
                       sem_send.at[3], sem_xh.at[s], g, wid(h, c)).start()
                remote(cot.at[c, :, :, lane(at)], cin.at[:, rows(local), lane(at)],
                       sem_send.at[4], sem_c.at[s], g, wid(h, c)).start()
            pltpu.make_async_copy(x.at[wc, :, lane(at)], xin.at[rows(m), lane(at + LANES)], sem_xh.at[s]).start()
            pltpu.make_async_copy(cot.at[wc, :, :, lane(at)], cin.at[:, rows(local), lane(at)], sem_c.at[s]).start()
            send_cond(s)

        here = pl.ds(pl.multiple_of(h * HALF, HALF), HALF)
        there = pl.ds(pl.multiple_of((1 - h) * HALF, HALF), HALF)

        def direct(s):
            at = s * sub
            for k in range(clips):
                c = lax.rem(wc + k, clips)
                remote(x.at[c, :, lane(at)], xin.at[rows(m), lane(at + LANES)],
                       sem_send.at[17], sem_xm.at[s], g, wid(1 - h, c)).start()

        far_rows = pl.ds(pl.multiple_of(h * (HALF + clips * r), r), HALF - clips * r)

        def relay(s):
            part = xin.at[far_rows, lane(s * sub + LANES)]
            drain(xin.at[here, lane(s * sub + LANES)], sem_xh.at[s])
            remote(part, part, sem_send.at[5], sem_xm.at[s], g, mirror).start()

            @pl.when(s + DIRECT < blocks)
            def _():
                direct(s + DIRECT)

            @pl.when(in_half(s))
            def _():
                also = cnd.at[pl.ds(0, mel), lane(s * sub)]
                drain(also, sem_k.at[s])
                remote(also, also, sem_send.at[12], sem_km.at[s], g, mirror).start()

        pl.loop(0, DIRECT)(direct)
        weights()
        pl.loop(0, AHEAD + OWN)(own)

        xin[:, 0:LANES] = jnp.zeros((RESIDUAL_WIDTH, LANES), BF)
        pg[...] = jnp.zeros_like(pg)
        cnd[mel:LANES, :] = (
            lax.broadcasted_iota(jnp.int32, (LANES - mel, slot), 0) == 0
        ).astype(F32).astype(BF)
        gacc[...] = jnp.zeros_like(gacc)
        csum[...] = jnp.zeros_like(csum)

        pl.loop(0, 2)(relay)
        drain(wall.at[kept, mine], sem_in.at[0])

        @pl.when(hub)
        def _():
            drain(wfw, sem_in.at[3])
            remote(wfw, wall.at[kept, mine], sem_send.at[2], sem_in.at[0], g, mirror).start()

        @pl.loop(1, d)
        def _(k):
            remote(wall.at[kept, mine], wall.at[kept, mine], sem_send.at[6], sem_in.at[1],
                   lax.rem(g + k, d), m).start()

        pl.loop(2, 9)(relay)
        drain(wall.at[kept, pl.ds(0, (d - 1) * piece)], sem_in.at[1])
        for k in range(1, clips):
            remote(wall.at[kept, :], wall.at[kept, :], sem_send.at[7], sem_in.at[2], g,
                   wid(h, lax.rem(wc + k, clips))).start()
        pl.loop(9, AHEAD)(relay)
        drain(wall.at[pl.ds(0, GH - band), :], sem_in.at[2])

        @pl.loop(0, USED // LANES)
        def _(i):
            wtr[pl.ds(pl.multiple_of(i * LANES, LANES), LANES), :] = wall[:, lane(i * LANES, LANES)].T

        length = lens[wc]

        def back(top):
            win = pg[...]
            pn = win[:, :sub]
            pe = pltpu.roll(win, sub + LANES - DILATION_STEP, 1)[:, :sub]

            def tap(base):
                return wtr[pl.ds(pl.multiple_of(base + top, HALF), HALF), :]

            return (dot(tap(512), pn[0:512]) + dot(wtr[pl.ds(pl.multiple_of(KP + 512 + top, LANES), HALF), :], pn[512:1024])
                    + dot(tap(0), pe[0:512]) + dot(wtr[pl.ds(pl.multiple_of(KP + top, LANES), HALF), :], pe[512:1024]))

        def gone(q):
            drain(gsend.at[:, pl.ds(0, sub)], sem_gv.at[lax.rem(q, POSTS)])

        def give(q):
            remote(gsend.at[:, lane((q + 1) * sub)], grecv.at[:, lane(q * sub)],
                   sem_gv.at[lax.rem(q, POSTS)], sem_gm.at[q], g, mirror).start()

        def add_cond(s):
            now = lane(s * sub)
            keeper = s // per
            spot = gco.at[wc, :, lane(s * sub - keeper * t)]
            drain(kr.at[:, now], sem_kr.at[s])
            gk[:, now] = (gk[:, now].astype(F32) + kr[:, now].astype(F32)).astype(BF)

            @pl.when(keeper == m)
            def _():
                pltpu.make_async_copy(gk.at[:, now], spot, sem_send.at[13]).start()

            @pl.when(keeper != m)
            def _():
                remote(gk.at[:, now], spot, sem_send.at[14], sem_in.at[6], g, keeper).start()

        def combine(q):
            now = lane(q * sub)
            z = lax.rem(q, SLOTS)
            drain(grecv.at[:, now], sem_gm.at[q])

            @pl.when(q >= SLOTS)
            def _():
                drain(gfs.at[z], sem_gf.at[z])

            gfs[z] = (gown[:, lane((q + 1) * sub)].astype(F32) + grecv[:, now].astype(F32)).astype(BF)

            @others
            def _(i):
                remote(gfs.at[z, rows(i), :], gio.at[wc, :, now], sem_gf.at[z], sem_in.at[5], g, first + i).start()

            pltpu.make_async_copy(gfs.at[z, rows(local), :], gio.at[wc, :, now], sem_gf.at[z]).start()

        def send_results(s):
            now = lane(s * sub)
            z = lax.rem(s, SLOTS)

            @others
            def _(i):
                remote(ost.at[z, :, rows(i), :], bro.at[wc, :, :, now], sem_o.at[z], sem_in.at[10], g, first + i).start()

            pltpu.make_async_copy(ost.at[z, :, rows(local), :], bro.at[wc, :, :, now], sem_o.at[z]).start()

            @pl.when(jnp.logical_not(in_half(s)))
            def _():
                remote(gk.at[:, now], kr.at[:, now], sem_send.at[8], sem_kr.at[s], g, mirror).start()

        @pl.loop(0, blocks)
        def _(s):
            at = s * sub
            now = lane(at)
            off = lane(at + LANES)
            z = lax.rem(s, SLOTS)

            @pl.when(s + AHEAD + OWN < blocks)
            def _():
                own(s + AHEAD + OWN)

            @pl.when(s + AHEAD < blocks)
            def _():
                relay(s + AHEAD)

            @pl.when(s >= 1)
            def _():
                send_results(s - 1)

            @pl.when(s >= GIVE + POSTS)
            def _():
                gone(s - GIVE - POSTS)

            @pl.when(s >= GIVE)
            def _():
                give(s - GIVE)

            @pl.when(s >= GIVE + LAG)
            def _():
                combine(s - GIVE - LAG)

            @pl.when(jnp.logical_and(s >= LATE, in_half(s - LATE)))
            def _():
                add_cond(s - LATE)

            @pl.when(jnp.logical_not(in_half(s)))
            def _():
                drain(cnd.at[pl.ds(0, mel), now], sem_km.at[s])

            @pl.when(s >= SLOTS)
            def _():
                drain(ost.at[z], sem_o.at[z])

            drain(xin.at[there, off], sem_xm.at[s])
            drain(cin.at[:, :, now], sem_c.at[s])

            xc = xin[:, off]
            xe = pltpu.roll(xin[:, lane(at, sub + LANES)], DILATION_STEP, 1)[:, LANES:]
            cd = cnd[:, now]
            pre_f = (dot(wall[:, 0:512], xe) + dot(wall[:, 512:1024], xc) + dot(wall[:, 1024:KP], cd))
            pre_g = (dot(wall[:, KP:KP + 512], xe) + dot(wall[:, KP + 512:KP + 1024], xc)
                     + dot(wall[:, KP + 1024:OUT_AT], cd))
            place = at + lax.broadcasted_iota(jnp.int32, (1, sub), 1)
            keep = (place < length).astype(F32)
            th = jnp.tanh(pre_f)
            sg = jax.nn.sigmoid(pre_g)
            hid = (keep * th * sg).astype(BF)
            branch = dot(wtr[OUT_AT:USED, :], hid)
            offset = wall[here, USED:USED + LANES].astype(F32)
            ost[z, 0] = (xin[here, off].astype(F32) + branch[0:HALF] + offset[:, 0:1]).astype(BF)
            ost[z, 1] = (branch[HALF:] + offset[:, 1:2]).astype(BF)
            ct = cin[:, :, now].reshape(2 * HALF, sub)
            for q in range(sub // LANES):
                csum[...] += ct[:, q * LANES:(q + 1) * LANES].astype(F32)
            hg = dot(wall[:, OUT_AT:USED], ct) * keep
            pgf = (hg * sg * (1.0 - th * th)).astype(BF)
            pgg = (hg * th * sg * (1.0 - sg)).astype(BF)
            pg[0:512, sub:] = pgf[:, :LANES]
            pg[512:1024, sub:] = pgg[:, :LANES]
            gacc[:, 0:512] += dot_nt(pgf, xe)
            gacc[:, 512:1024] += dot_nt(pgf, xc)
            gacc[:, 1024:KP] += dot_nt(pgf, cd)
            gacc[:, KP:KP + 512] += dot_nt(pgg, xe)
            gacc[:, KP + 512:KP + 1024] += dot_nt(pgg, xc)
            gacc[:, KP + 1024:OUT_AT] += dot_nt(pgg, cd)
            gacc[:, OUT_AT:USED] += dot_nt(hid, ct)
            gk[:, now] = (dot(wtr[1024:KP, :], pgf) + dot(wtr[KP + 1024:OUT_AT, :], pgg))[0:mel].astype(BF)
            gsend[:, now] = back((1 - h) * HALF).astype(BF)
            gown[:, now] = back(h * HALF).astype(BF)
            pg[0:512, 0:sub] = pgf
            pg[512:1024, 0:sub] = pgg

        send_results(blocks - 1)
        pg[:, sub:] = jnp.zeros((2 * GH, LANES), BF)
        gsend[:, pl.ds(slot, sub)] = back((1 - h) * HALF).astype(BF)
        gown[:, pl.ds(slot, sub)] = back(h * HALF).astype(BF)

        def spread(part, dst, sem):
            @others
            def _(i):
                remote(part.at[rows(i), :], dst, sem, sem_in.at[8], g, first + i).start()

            pltpu.make_async_copy(part.at[rows(local), :], dst, sem_in.at[8]).start()

        spot = lax.broadcasted_iota(jnp.int32, (HALF, LANES), 1)
        total = jnp.sum(csum[...], axis=1, keepdims=True)
        gacc[here, USED:USED + LANES] = jnp.where(spot == 0, total[0:HALF], jnp.where(spot == 1, total[HALF:], 0.0))

        s0 = cin.at[0, :, pl.ds(0, WIDE)]
        for k in range(1, clips):
            to = lax.rem(wc + k, clips)
            s0[...] = gacc[pl.ds(pl.multiple_of(to * band, band), band), :].astype(BF)
            remote(s0, r0.at[k - 1], sem_send.at[9], sem_in.at[7], g, wid(h, to)).start()

        start = blocks - GIVE
        pl.loop(start - POSTS, start - SLOTS)(gone)

        def tail(q):
            gone(q - SLOTS)
            give(q)
            combine(q - LAG)
            more = q + GIVE - LATE

            @pl.when(jnp.logical_and(more < blocks, in_half(more)))
            def _():
                add_cond(more)

        pl.loop(start, start + 2)(tail)
        drain(r0, sem_in.at[7])
        for k in range(1, clips):
            gacc[kept, :] += r0[k - 1].astype(F32)

        @pl.loop(1, d)
        def _(k):
            to = lax.rem(g + k, d)
            src = cin.at[1, :, lane((k - 1) * piece, piece)]
            src[...] = gacc[kept, lane(to * piece, piece)].astype(BF)
            remote(src, r1.at[k - 1], sem_send.at[10], sem_r1.at[k - 1], to, m).start()

        pl.loop(start + 2, start + 7)(tail)

        @pl.loop(1, d)
        def _(k):
            drain(r1.at[k - 1], sem_r1.at[k - 1])
            gacc[kept, mine] += r1[k - 1].astype(F32)

        s2[...] = gacc[kept, mine].astype(BF)

        @pl.when(jnp.logical_not(hub))
        def _():
            remote(s2, r2, sem_send.at[11], sem_in.at[4], g, mirror).start()

        pl.loop(start + 7, start + 13)(tail)

        @pl.when(hub)
        def _():
            drain(r2, sem_in.at[4])

            @pl.when(shared)
            def _():
                s2[...] = (gacc[kept, mine] + r2[...].astype(F32)).astype(BF)
                spread(s2, gw.at[0, :, mine], sem_send.at[11])

            @pl.when(jnp.logical_not(shared))
            def _():
                spread(s2, gw.at[h, :, mine], sem_send.at[11])
                spread(r2, gw.at[1 - h, :, mine], sem_send.at[15])

        pl.loop(start + 13, blocks)(tail)
        share_out()
        pl.loop(blocks - SLOTS, blocks)(gone)
        pl.loop(blocks - LAG, blocks)(combine)

        @pl.loop(0, SLOTS)
        def _(q):
            drain(ost.at[q], sem_o.at[q])
            drain(gfs.at[q], sem_gf.at[q])

        drain(x.at[pl.ds(0, clips - 1)], sem_send.at[3])
        drain(cot.at[pl.ds(0, clips - 1)], sem_send.at[4])
        drain(xin.at[pl.ds(0, HALF - clips * r), pl.ds(0, slot)], sem_send.at[5])
        drain(x, sem_send.at[17])
        drain(wall.at[kept, pl.ds(0, (d - 1) * piece)], sem_send.at[6])
        drain(wall.at[pl.ds(0, GH - band), :], sem_send.at[7])
        drain(gk.at[:, pl.ds(0, slot // 2)], sem_send.at[8])
        drain(cnd.at[pl.ds(0, mel), pl.ds(0, slot // 2)], sem_send.at[12])
        drain(gk.at[:, pl.ds(0, t)], sem_send.at[13])
        drain(gk.at[:, pl.ds(0, slot // 2 - t)], sem_send.at[14])
        drain(r0, sem_send.at[9])
        drain(r1, sem_send.at[10])

    def share_out():
        @pl.when(shared)
        def _():
            drain(gw.at[0, :, mine], sem_in.at[8])
            share(gw.at[0, :, mine])

        @pl.when(jnp.logical_not(shared))
        def _():
            drain(gw.at[:, :, mine], sem_in.at[8])
            share(gw.at[:, :, mine])

    def share(part):
        @pl.loop(1, d)
        def _(k):
            remote(part, part, sem_send.at[16], sem_in.at[9], lax.rem(g + k, d), m).start()

    @pl.when(worker)
    def _():
        work()
        drain(cond.at[pl.ds(0, clips - 1)], sem_send.at[0])
        drain(bro.at[pl.ds(0, clips - 1)], sem_in.at[10])
        drain(gio.at[pl.ds(0, clips - 1)], sem_in.at[5])
        drain(gco.at[pl.ds(0, clips - 1)], sem_in.at[6])

        @pl.when(hub)
        def _():
            drain(wfw, sem_send.at[2])
            drain(s2.at[pl.ds(0, HALF - r), :], sem_send.at[11])

            @pl.when(jnp.logical_not(shared))
            def _():
                drain(r2.at[pl.ds(0, HALF - r), :], sem_send.at[15])

        @pl.when(jnp.logical_not(hub))
        def _():
            drain(wcat.at[:, :, mine], sem_send.at[1])
            drain(s2, sem_send.at[11])

    @pl.when(jnp.logical_not(worker))
    def _():
        far()
        share_out()
        drain(cond, sem_send.at[0])
        drain(wcat.at[:, :, mine], sem_send.at[1])
        drain(bro, sem_in.at[10])
        drain(gio, sem_in.at[5])
        drain(gco, sem_in.at[6])

    own_piece = 2 * d - OUT_AT // piece

    @pl.when(shared)
    def _():
        whole(gw, own_piece - 1, sem_in.at[9])
        whole(gw, d - 1, sem_send.at[16])

    @pl.when(jnp.logical_not(shared))
    def _():
        whole(gw, own_piece - 2, sem_in.at[9])
        whole(gw, 2 * (d - 1), sem_send.at[16])


def run_layer(n, d, x, cot, cond, lens, wcat):
    clips, r, slot = x.shape
    mel = cond.shape[1]
    t = slot // n
    sub = min(256, t)
    blocks = slot // sub
    piece = WIDE // d
    width = RESIDUAL_WIDTH
    band = GH // clips
    any_spec = pl.BlockSpec(memory_space=pl.ANY)
    vmem = pl.BlockSpec(memory_space=pltpu.VMEM)
    smem = pl.BlockSpec(memory_space=pltpu.SMEM)
    dma = pltpu.SemaphoreType.DMA
    return pl.pallas_call(
        functools.partial(layer_kernel, n, d, clips, slot, sub, mel),
        out_shape=(
            jax.ShapeDtypeStruct((clips, 2, r, slot), BF),
            jax.ShapeDtypeStruct((clips, r, slot), BF),
            jax.ShapeDtypeStruct((clips, mel, t), BF),
            jax.ShapeDtypeStruct((2, r, WIDE), BF),
        ),
        in_specs=[any_spec, any_spec, any_spec, smem, vmem],
        out_specs=(any_spec, any_spec, any_spec, vmem),
        scratch_shapes=[
            pltpu.VMEM((width, LANES + slot), BF),
            pltpu.VMEM((2, HALF, slot), BF),
            pltpu.VMEM((LANES, slot), BF),
            pltpu.VMEM((HALF, slot), BF),
            pltpu.VMEM((HALF, slot + sub), BF),
            pltpu.VMEM((HALF, slot + sub), BF),
            pltpu.VMEM((GH, WIDE), BF),
            pltpu.VMEM((HALF, piece), BF),
            pltpu.VMEM((USED, GH), BF),
            pltpu.VMEM((2 * GH, sub + LANES), BF),
            pltpu.VMEM((GH, WIDE), F32),
            pltpu.VMEM((2 * HALF, LANES), F32),
            pltpu.VMEM((SLOTS, 2, HALF, sub), BF),
            pltpu.VMEM((SLOTS, HALF, sub), BF),
            pltpu.VMEM((mel, slot), BF),
            pltpu.VMEM((mel, slot), BF),
            pltpu.VMEM((clips - 1, band, WIDE), BF),
            pltpu.VMEM((d - 1, band, piece), BF),
            pltpu.VMEM((band, piece), BF),
            pltpu.VMEM((band, piece), BF),
            dma((SLOTS,)),
            dma((SLOTS,)),
            dma((18,)),
            dma((blocks,)),
            dma((blocks,)),
            dma((blocks,)),
            dma((blocks,)),
            dma((blocks,)),
            dma((blocks,)),
            dma((blocks,)),
            dma((POSTS,)),
            dma((SLOTS,)),
            dma((SLOTS,)),
            dma((11,)),
            dma((d - 1,)),
        ],
        compiler_params=pltpu.CompilerParams(
            collective_id=0, has_side_effects=True, vmem_limit_bytes=60 << 20
        ),
    )(x, cot, cond, lens, wcat)


def adamw(master, first_old, second_old, gradient, step_rate, power_one, power_two):
    first_new = BETA_ONE * first_old + (1.0 - BETA_ONE) * gradient
    second_new = BETA_TWO * second_old + (1.0 - BETA_TWO) * gradient * gradient
    first_hat = first_new / (1.0 - power_one)
    second_hat = second_new / (1.0 - power_two)
    renewed = master - step_rate * (
        first_hat / (jnp.sqrt(second_hat) + EPSILON) + WEIGHT_DECAY * master
    )
    return (renewed, first_new, second_new)


def per_device(
    n, d,
    inputs, conditioning, lengths, cotangent, conv_weight, out_weight, biases,
    conv_first, out_first, bias_first, conv_second, out_second, bias_second,
):
    clips, r, slot = inputs.shape
    taps = conv_weight.shape[0]
    bias_low = biases.astype(BF)
    flipped = jnp.transpose(conv_weight.astype(BF), (1, 2, 0))
    flipped = jnp.concatenate(
        [flipped, bias_low[0:2, :, None], jnp.zeros((2, r, KP - taps - 1), BF)], axis=2
    )
    out_low = out_weight.astype(BF).reshape(r, 2, 2, HALF)
    wcat = jnp.stack(
        [
            jnp.concatenate(
                [
                    flipped[0],
                    flipped[1],
                    out_low[:, 0, side],
                    out_low[:, 1, side],
                    bias_low[2:4].T,
                    jnp.zeros((r, WIDE - USED - 2), BF),
                ],
                axis=1,
            )
            for side in range(2)
        ],
        axis=0,
    )
    cond = jnp.transpose(conditioning, (0, 2, 1))
    layer_out, gio, gco, gw = run_layer(n, d, inputs, cotangent, cond, lengths, wcat)

    grad_input = cotangent[:, 0].astype(F32) + gio.astype(F32)
    grad_cond = jnp.transpose(gco.astype(F32), (0, 2, 1))
    gsum = gw[0].astype(F32)
    both = gsum[:, USED : USED + 2] + gw[1, :, USED : USED + 2].astype(F32)
    conv_grad = jnp.transpose(
        jnp.stack([gsum[:, :taps], gsum[:, KP : KP + taps]], axis=0), (2, 0, 1)
    )
    out_grad = jnp.stack(
        [gw[:, :, OUT_AT : OUT_AT + HALF], gw[:, :, OUT_AT + HALF : USED]], axis=0
    )
    out_grad = jnp.transpose(out_grad, (2, 0, 1, 3)).reshape(r, 4 * HALF).astype(F32)
    bias_grad = jnp.stack(
        [gsum[:, taps], gsum[:, KP + taps], both[:, 0], both[:, 1]], axis=0
    )
    power_one = jnp.float32(BETA_ONE**STEP)
    power_two = jnp.float32(BETA_TWO**STEP)
    conv_new = adamw(
        conv_weight, conv_first, conv_second, conv_grad, CONV_RATE, power_one, power_two
    )
    out_new = adamw(out_weight, out_first, out_second, out_grad, OUT_RATE, power_one, power_two)
    bias_new = adamw(biases, bias_first, bias_second, bias_grad, BIAS_RATE, power_one, power_two)
    return (
        layer_out,
        grad_input,
        grad_cond,
        conv_new[0],
        out_new[0],
        bias_new[0],
        conv_new[1],
        out_new[1],
        bias_new[1],
        conv_new[2],
        out_new[2],
        bias_new[2],
        conv_new[0].astype(BF),
        out_new[0].astype(BF),
        bias_new[0].astype(BF),
    )


def solution(mesh):
    in_specs = (
        P("dp", "mp", None),
        P("dp", "mp", None),
        P("dp"),
        P("dp", None, "mp", None),
        P(None, None, "mp"),
        P("mp", None),
        P(None, "mp"),
        P(None, None, "mp"),
        P("mp", None),
        P(None, "mp"),
        P(None, None, "mp"),
        P("mp", None),
        P(None, "mp"),
    )
    out_specs = (
        P("dp", None, "mp", None),
        P("dp", "mp", None),
        P("dp", "mp", None),
        P(None, None, "mp"),
        P("mp", None),
        P(None, "mp"),
        P(None, None, "mp"),
        P("mp", None),
        P(None, "mp"),
        P(None, None, "mp"),
        P("mp", None),
        P(None, "mp"),
        P(None, None, "mp"),
        P("mp", None),
        P(None, "mp"),
    )
    return jax.shard_map(
        functools.partial(per_device, mesh.shape["mp"], mesh.shape["dp"]),
        mesh=mesh, in_specs=in_specs, out_specs=out_specs, check_vma=False,
    )
```

time: 275 us -> 256 us (0.931)
  Pallas kernels: 249 us -> 235 us
  other arithmetic: 18.8 us -> 12.9 us
    pallas_call x1, Pallas kernels: 249 us -> 235 us  [run_layer(): pl.pallas_call(functools.partial(layer_kernel, n, d, clips, slot, sub, me...]
    another operation x3 -> x0, other arithmetic: 5.36 us -> none  [the longest x2 3.14 us: per_device(): jnp.stack([inputs.astype(F32) + bro[:, 0].astype(F32) + bias_out[0][None,...]
    reduce_sum x2 -> x0, other arithmetic: 2.9 us -> none  [the longest x1 2.89 us: per_device(): sums = jnp.sum(cotangent.astype(F32), axis=(0, 3))]
where the time goes in v3:
time: 256 us
  Pallas kernels  235 us (92%)
  other arithmetic  12.9 us (5%)
  local copies, waits for them, and re-layouts  6.91 us (3%)
    pallas_call x1, Pallas kernels, run_layer(): pl.pallas_call(functools.partial(layer_kernel, n, d, clips, slot, sub, me...  235 us

profile of v3, /device:TPU:0, one launch (start us, length us, event | category | flops | bytes accessed | tf_op | source)
XLA Modules:
  0.0 255.5 jit_solution(15914932214675316504)
XLA Ops:
  0.6 1.1 convert_bitcast_fusion.1
  1.7 0.7 convert_element_type.50
  2.4 0.1 copy.62
  2.6 0.5 copy.49
  3.1 0.1 concatenate.9
  3.3 1.0 convert_element_type.51
  4.2 0.1 reshape.42
  4.3 0.2 fusion.9
  4.5 0.1 copy.52
  4.6 0.1 concatenate.11
  4.8 0.1 concatenate.10
  4.8 1.0 pad_maximum_fusion.wcat
  5.8 234.8 %shard_map.244 = (bf16[2,2,64,8192]{3,2,1,0:T(8,128)(2,1)}, bf16[2,64,8192]{2,1,0:T(8,128)(2,1)}, bf16[2,80,1024]{2,1,0:T(8,128)(2,1)}, bf16[2,64,3072]{2,1,0:T(8,128)(2,1)}) custom-call(bf16[2,64,8192]{2,1,0:T(8,128)(2,1)} %x.1, bf16[2,2,64,8192]{3,2,1,0:T(8,128)(2,1)} %cot.1, bf16[2,80,1024]{2,1,0:T(8,128)(2,1)} %bitcast.56, s32[2]{0:T(128)} %lens.1, ...), custom_call_target="tpu_custom_call" | custom-call | tf_op jit(solution)/shard_map/pallas_call | solution.py:595
  240.6 0.0 copy-start.5
  240.6 0.0 copy-start
  240.7 0.0 copy-start.2
  240.7 0.0 copy-start.3
  240.7 4.9 %convert_add_fusion = f32[2,64,8192]{2,1,0:T(8,128)} fusion(bf16[2,64,8192]{2,1,0:T(8,128)(2,1)} %get-tuple-element.20, bf16[2,2,64,8192]{3,2,1,0:T(8,128)(2,1)} %cot.1), kind=kLoop, calls=%fused_computation | loop fusion | flops 3145728 | bytes 8388608 | tf_op jit(solution)/shard_map/add | solution.py:692
  245.6 0.9 convert_bitcast_fusion
  246.5 0.0 copy-done.4
  246.5 0.1 bitcast_convert_fusion
  246.6 0.0 copy-start.8
  246.6 0.0 copy-start.9
  246.6 0.0 copy-start.10
  246.7 1.6 fusion.7
  248.3 0.2 copy.56
  248.6 0.2 reshape.45
  248.8 1.0 fusion.5
  249.9 0.2 slice_reduce_fusion.1
  250.0 0.2 slice_reduce_fusion.3
  250.3 0.6 fusion.3
  250.9 4.6 %copy.73 = bf16[2,2,64,8192]{3,2,1,0:T(8,128)(2,1)} copy(bf16[2,2,64,8192]{3,2,1,0:T(8,128)(2,1)} %get-tuple-element.70) | data formatting | bytes 8388608
  (24 shorter events, 0.2 us)
Async XLA Ops:
  240.6 5.0 %copy-start.5 = (bf16[2,80,1024]{2,1,0:T(8,128)(2,1)S(1)}, bf16[2,80,1024]{2,1,0:T(8,128)(2,1)}, u32[]{:S(2)}) copy-start(bf16[2,80,1024]{2,1,0:T(8,128)(2,1)} %get-tuple-element.21) | copy-start | bytes 983044
  240.6 5.9 %copy-start.4 = (bf16[2,64,3072]{2,1,0:T(8,128)(2,1)S(1)}, bf16[2,64,3072]{2,1,0:T(8,128)(2,1)}, u32[]{:S(2)}) copy-start(bf16[2,64,3072]{2,1,0:T(8,128)(2,1)} %get-tuple-element.22) | copy-start | bytes 2359300
  240.6 6.0 %copy-start = (f32[1104,2,64]{0,2,1:T(8,128)S(1)}, f32[1104,2,64]{0,2,1:T(8,128)}, u32[]{:S(2)}) copy-start(f32[1104,2,64]{0,2,1:T(8,128)} %param.17) | copy-start | bytes 1695748
  240.7 6.0 %copy-start.2 = (f32[1104,2,64]{0,2,1:T(8,128)S(1)}, f32[1104,2,64]{0,2,1:T(8,128)}, u32[]{:S(2)}) copy-start(f32[1104,2,64]{0,2,1:T(8,128)} %param.20) | copy-start | bytes 1695748
  240.7 6.0 %copy-start.3 = (f32[1104,2,64]{0,2,1:T(8,128)S(1)}, f32[1104,2,64]{0,2,1:T(8,128)}, u32[]{:S(2)}) copy-start(f32[1104,2,64]{0,2,1:T(8,128)} %param.23) | copy-start | bytes 1695748
  246.5 2.3 copy-start.1
  246.5 2.3 copy-start.6
  246.5 2.3 copy-start.7
  246.6 3.6 %copy-start.8 = (f32[4,64]{1,0:T(4,128)S(1)}, f32[4,64]{1,0:T(4,128)}, u32[]{:S(2)}) copy-start(f32[4,64]{1,0:T(4,128)} %param.19) | copy-start | bytes 3076
  246.6 3.6 %copy-start.9 = (f32[4,64]{1,0:T(4,128)S(1)}, f32[4,64]{1,0:T(4,128)}, u32[]{:S(2)}) copy-start(f32[4,64]{1,0:T(4,128)} %param.22) | copy-start | bytes 3076
  246.6 3.6 %copy-start.10 = (f32[4,64]{1,0:T(4,128)S(1)}, f32[4,64]{1,0:T(4,128)}, u32[]{:S(2)}) copy-start(f32[4,64]{1,0:T(4,128)} %param.25) | copy-start | bytes 3076

commit v4 on v3

--- a/solution.py
+++ b/solution.py
@@ -49,10 +49,10 @@
 
 def layer_kernel(
     n, d, clips, slot, sub, mel,
-    x, cot, cond, lens, wcat,
+    x, cot, cond, lens, conv, proj, bias,
     bro, gio, gco, gw,
-    xin, cin, cnd, grecv, gsend, gown, wall, wfw, wtr, pg, gacc, csum, ost, gfs, gk, kr, r0, r1, s2, r2,
-    sem_fx, sem_fc, sem_send, sem_xh, sem_xm, sem_c, sem_k, sem_km, sem_kr, sem_gm, sem_gv, sem_o, sem_gf, sem_in, sem_r1,
+    convf, turn, xin, cin, cnd, grecv, gsend, gown, wall, wtr, pg, gacc, csum, ost, gfs, gk, kr, r0, r1, s2, r2,
+    sem_fx, sem_fc, sem_send, sem_xh, sem_xm, sem_c, sem_k, sem_km, sem_kr, sem_gm, sem_gv, sem_o, sem_gf, sem_in, sem_r1, sem_pre,
 ):
     g = lax.axis_index("dp")
     m = lax.axis_index("mp")
@@ -100,6 +100,10 @@
     def whole(ref, count, sem):
         drain(ref.at[0, :, pl.ds(0, count * piece)] if count <= d else ref.at[:, :, pl.ds(0, count // 2 * piece)], sem)
 
+    projf = gacc.at[pl.ds(0, r), pl.ds(0, proj.shape[1])]
+    pltpu.make_async_copy(conv, convf, sem_pre.at[0]).start()
+    pltpu.make_async_copy(proj, projf, sem_pre.at[1]).start()
+
     bar = pltpu.get_barrier_semaphore()
 
     @pl.loop(1, half)
@@ -121,6 +125,12 @@
         pl.semaphore_wait(bar, half + d - 2)
 
     mine = lane(g * piece, piece)
+
+    def laid(hh):
+        return gsend.at[rows(hh), pl.ds(0, WIDE)]
+
+    def laid_piece(hh):
+        return gsend.at[rows(hh), mine]
     kept = pl.ds(pl.multiple_of(wc * band, band), band)
 
     def send_cond(s):
@@ -139,19 +149,44 @@
                 def _():
                     remote(part, dst, sem_send.at[0], sem_k.at[s], g, to).start()
 
+    def later(s):
+        return lane(lax.rem(s, blocks // 2) * sub)
+
     def in_half(s):
         return s // (blocks // 2) == h
 
     def weights():
+        taps = convf.shape[2]
+        drain(convf, sem_pre.at[0])
+        drain(projf, sem_pre.at[1])
+        wide = projf[...]
+        turn[...] = jnp.zeros_like(turn)
+        turn[0:4, 0:r] = bias[...]
+        column = turn[...].T
+        spot = lax.broadcasted_iota(jnp.int32, (r, LANES), 1)
+        for hh in range(2):
+            form = laid(hh)
+            for q in range(2):
+                base = q * KP
+                form[:, base:base + 1024] = convf[q, :, 0:1024].astype(BF)
+                form[:, base + 1024:base + KP] = jnp.where(
+                    spot == taps - 1024, column[0:r, q:q + 1], 0.0).astype(BF)
+                form[:, base + 1024:base + taps] = convf[q, :, 1024:taps].astype(BF)
+                form[:, OUT_AT + q * HALF:OUT_AT + (q + 1) * HALF] = wide[
+                    :, (2 * q + hh) * HALF:(2 * q + hh + 1) * HALF].astype(BF)
+            form[:, USED:USED + LANES] = jnp.where(
+                spot == 0, column[0:r, 2:3], jnp.where(spot == 1, column[0:r, 3:4], 0.0)).astype(BF)
+            form[:, USED + LANES:] = jnp.zeros((r, WIDE - USED - LANES), BF)
+
         @pl.when(hub)
         def _():
-            pltpu.make_async_copy(wcat.at[h, :, mine], wall.at[rows(m), mine], sem_in.at[0]).start()
-            pltpu.make_async_copy(wcat.at[1 - h, :, mine], wfw.at[rows(local), :], sem_in.at[3]).start()
+            pltpu.make_async_copy(laid_piece(h), wall.at[rows(m), mine], sem_in.at[0]).start()
+            pltpu.make_async_copy(laid_piece(1 - h), s2.at[rows(local), :], sem_in.at[3]).start()
 
         @pl.when(jnp.logical_not(hub))
         def _():
-            remote(wcat.at[h, :, mine], wall.at[rows(m), mine], sem_send.at[1], sem_in.at[0], g, wid(h, h)).start()
-            remote(wcat.at[1 - h, :, mine], wfw.at[rows(local), :], sem_send.at[1], sem_in.at[3], g, wid(h, h)).start()
+            remote(laid_piece(h), wall.at[rows(m), mine], sem_send.at[1], sem_in.at[0], g, wid(h, h)).start()
+            remote(laid_piece(1 - h), s2.at[rows(local), :], sem_send.at[1], sem_in.at[3], g, wid(h, h)).start()
 
     def far():
         def send_x(s):
@@ -251,8 +286,8 @@
 
         @pl.when(hub)
         def _():
-            drain(wfw, sem_in.at[3])
-            remote(wfw, wall.at[kept, mine], sem_send.at[2], sem_in.at[0], g, mirror).start()
+            drain(s2, sem_in.at[3])
+            remote(s2, wall.at[kept, mine], sem_send.at[2], sem_in.at[0], g, mirror).start()
 
         @pl.loop(1, d)
         def _(k):
@@ -267,6 +302,15 @@
         pl.loop(9, AHEAD)(relay)
         drain(wall.at[pl.ds(0, GH - band), :], sem_in.at[2])
 
+        @pl.when(hub)
+        def _():
+            drain(s2, sem_send.at[2])
+
+        @pl.when(jnp.logical_not(hub))
+        def _():
+            drain(gsend.at[pl.ds(0, 2 * r), mine], sem_send.at[1])
+
+
         @pl.loop(0, USED // LANES)
         def _(i):
             wtr[pl.ds(pl.multiple_of(i * LANES, LANES), LANES), :] = wall[:, lane(i * LANES, LANES)].T
@@ -295,8 +339,8 @@
             now = lane(s * sub)
             keeper = s // per
             spot = gco.at[wc, :, lane(s * sub - keeper * t)]
-            drain(kr.at[:, now], sem_kr.at[s])
-            gk[:, now] = (gk[:, now].astype(F32) + kr[:, now].astype(F32)).astype(BF)
+            drain(kr.at[:, later(s)], sem_kr.at[s])
+            gk[:, now] = (gk[:, now].astype(F32) + kr[:, later(s)].astype(F32)).astype(BF)
 
             @pl.when(keeper == m)
             def _():
@@ -335,7 +379,7 @@
 
             @pl.when(jnp.logical_not(in_half(s)))
             def _():
-                remote(gk.at[:, now], kr.at[:, now], sem_send.at[8], sem_kr.at[s], g, mirror).start()
+                remote(gk.at[:, now], kr.at[:, later(s)], sem_send.at[8], sem_kr.at[s], g, mirror).start()
 
         @pl.loop(0, blocks)
         def _(s):
@@ -544,7 +588,6 @@
 
         @pl.when(hub)
         def _():
-            drain(wfw, sem_send.at[2])
             drain(s2.at[pl.ds(0, HALF - r), :], sem_send.at[11])
 
             @pl.when(jnp.logical_not(shared))
@@ -553,7 +596,6 @@
 
         @pl.when(jnp.logical_not(hub))
         def _():
-            drain(wcat.at[:, :, mine], sem_send.at[1])
             drain(s2, sem_send.at[11])
 
     @pl.when(jnp.logical_not(worker))
@@ -561,7 +603,7 @@
         far()
         share_out()
         drain(cond, sem_send.at[0])
-        drain(wcat.at[:, :, mine], sem_send.at[1])
+        drain(gsend.at[pl.ds(0, 2 * r), mine], sem_send.at[1])
         drain(bro, sem_in.at[10])
         drain(gio, sem_in.at[5])
         drain(gco, sem_in.at[6])
@@ -579,7 +621,7 @@
         whole(gw, 2 * (d - 1), sem_send.at[16])
 
 
-def run_layer(n, d, x, cot, cond, lens, wcat):
+def run_layer(n, d, x, cot, cond, lens, conv, proj, bias):
     clips, r, slot = x.shape
     mel = cond.shape[1]
     t = slot // n
@@ -588,7 +630,7 @@
     piece = WIDE // d
     width = RESIDUAL_WIDTH
     band = GH // clips
-    any_spec = pl.BlockSpec(memory_space=pl.ANY)
+    any_spec = pl.BlockSpec(memory_space=pltpu.HBM)
     vmem = pl.BlockSpec(memory_space=pltpu.VMEM)
     smem = pl.BlockSpec(memory_space=pltpu.SMEM)
     dma = pltpu.SemaphoreType.DMA
@@ -600,9 +642,11 @@
             jax.ShapeDtypeStruct((clips, mel, t), BF),
             jax.ShapeDtypeStruct((2, r, WIDE), BF),
         ),
-        in_specs=[any_spec, any_spec, any_spec, smem, vmem],
+        in_specs=[any_spec, any_spec, any_spec, smem, any_spec, any_spec, vmem],
         out_specs=(any_spec, any_spec, any_spec, vmem),
         scratch_shapes=[
+            pltpu.VMEM(conv.shape, F32),
+            pltpu.VMEM((8, LANES), F32),
             pltpu.VMEM((width, LANES + slot), BF),
             pltpu.VMEM((2, HALF, slot), BF),
             pltpu.VMEM((LANES, slot), BF),
@@ -610,7 +654,6 @@
             pltpu.VMEM((HALF, slot + sub), BF),
             pltpu.VMEM((HALF, slot + sub), BF),
             pltpu.VMEM((GH, WIDE), BF),
-            pltpu.VMEM((HALF, piece), BF),
             pltpu.VMEM((USED, GH), BF),
             pltpu.VMEM((2 * GH, sub + LANES), BF),
             pltpu.VMEM((GH, WIDE), F32),
@@ -618,7 +661,7 @@
             pltpu.VMEM((SLOTS, 2, HALF, sub), BF),
             pltpu.VMEM((SLOTS, HALF, sub), BF),
             pltpu.VMEM((mel, slot), BF),
-            pltpu.VMEM((mel, slot), BF),
+            pltpu.VMEM((mel, slot // 2), BF),
             pltpu.VMEM((clips - 1, band, WIDE), BF),
             pltpu.VMEM((d - 1, band, piece), BF),
             pltpu.VMEM((band, piece), BF),
@@ -638,11 +681,12 @@
             dma((SLOTS,)),
             dma((11,)),
             dma((d - 1,)),
+            dma((2,)),
         ],
         compiler_params=pltpu.CompilerParams(
             collective_id=0, has_side_effects=True, vmem_limit_bytes=60 << 20
         ),
-    )(x, cot, cond, lens, wcat)
+    )(x, cot, cond, lens, conv, proj, bias)
 
 
 def adamw(master, first_old, second_old, gradient, step_rate, power_one, power_two):
@@ -656,77 +700,166 @@
     return (renewed, first_new, second_new)
 
 
+def finish_kernel(
+    taps, span,
+    lo, gio, cot, gco, gw, cw, cm, cv, ow, om, ov, bw, bm, bv,
+    lo_out, gi_out, gc_out, cw_out, ow_out, bw_out, cm_out, om_out, bm_out, cv_out, ov_out, bv_out,
+    cl_out, ol_out, bl_out,
+    lo_v, gio_v, cot_v, gi_v, gco_v, gc_v, gw_v, conv_v, convl_v, proj_v, projl_v,
+    sem_lo, sem_gi, sem_cot, sem_small, sem_out,
+):
+    clips, r, slot = gio.shape
+    parts = slot // span
+    power_one = jnp.float32(BETA_ONE**STEP)
+    power_two = jnp.float32(BETA_TWO**STEP)
+
+    small = [
+        pltpu.make_async_copy(src, dst, sem_small.at[i])
+        for i, (src, dst) in enumerate(
+            [(gw, gw_v), (gco, gco_v)]
+            + [(a, conv_v.at[q]) for q, a in enumerate((cw, cm, cv))]
+            + [(a, proj_v.at[q]) for q, a in enumerate((ow, om, ov))]
+        )
+    ]
+    blocks = [(c, slice(p * span, (p + 1) * span)) for c in range(clips) for p in range(parts)]
+    loads = [
+        (
+            pltpu.make_async_copy(gio.at[c, :, at], gio_v.at[c, :, at], sem_gi.at[i]),
+            pltpu.make_async_copy(cot.at[c, 0, :, at], cot_v.at[c, :, at], sem_cot.at[i]),
+            pltpu.make_async_copy(lo.at[c, :, :, at], lo_v.at[c, :, :, at], sem_lo.at[i]),
+        )
+        for i, (c, at) in enumerate(blocks)
+    ]
+    for copy in small[:5]:
+        copy.start()
+    for load in loads[:2]:
+        for copy in load:
+            copy.start()
+    for copy in small[5:]:
+        copy.start()
+    for load in loads[2:]:
+        for copy in load:
+            copy.start()
+
+    stores = []
+
+    def store(src, dst):
+        copy = pltpu.make_async_copy(src, dst, sem_out.at[len(stores)])
+        copy.start()
+        stores.append(copy)
+
+    def block(i):
+        c, at = blocks[i]
+        one, two, three = loads[i]
+        three.wait()
+        store(lo_v.at[c, :, :, at], lo_out.at[c, :, :, at])
+        one.wait()
+        two.wait()
+        gi_v[c, :, at] = cot_v[c, :, at].astype(F32) + gio_v[c, :, at].astype(F32)
+        store(gi_v.at[c, :, at], gi_out.at[c, :, at])
+
+    block(0)
+    for copy in small[:5]:
+        copy.wait()
+    gc_v[...] = gco_v[...].astype(F32)
+    store(gc_v, gc_out)
+    for q in range(2):
+        w, m, v = adamw(conv_v[0, q], conv_v[1, q], conv_v[2, q], gw_v[0, :, q * KP:q * KP + taps].astype(F32),
+                        CONV_RATE, power_one, power_two)
+        conv_v[0, q], conv_v[1, q], conv_v[2, q] = w, m, v
+        convl_v[q] = w.astype(BF)
+    for i, dst in enumerate((cw_out, cm_out, cv_out)):
+        store(conv_v.at[i], dst)
+    store(convl_v, cl_out)
+    block(1)
+    for copy in small[5:]:
+        copy.wait()
+    for q in range(4):
+        at = slice(q * HALF, (q + 1) * HALF)
+        from_at = OUT_AT + q // 2 * HALF
+        w, m, v = adamw(proj_v[0, :, at], proj_v[1, :, at], proj_v[2, :, at],
+                        gw_v[q % 2, :, from_at:from_at + HALF].astype(F32), OUT_RATE, power_one, power_two)
+        proj_v[0, :, at], proj_v[1, :, at], proj_v[2, :, at] = w, m, v
+        projl_v[:, at] = w.astype(BF)
+    for i, dst in enumerate((ow_out, om_out, ov_out)):
+        store(proj_v.at[i], dst)
+    store(projl_v, ol_out)
+    spot = lax.broadcasted_iota(jnp.int32, (r, LANES), 1)
+    last = taps - 1024
+    sums = gw_v[0, :, USED:USED + LANES].astype(F32) + gw_v[1, :, USED:USED + LANES].astype(F32)
+    columns = (
+        gw_v[0, :, 1024:KP].astype(F32)[:, last:last + 1],
+        gw_v[0, :, KP + 1024:OUT_AT].astype(F32)[:, last:last + 1],
+        sums[:, 0:1],
+        sums[:, 1:2],
+    )
+    table = jnp.zeros((r, LANES), F32)
+    for i, column in enumerate(columns):
+        table = jnp.where(spot == i, column, table)
+    w, m, v = adamw(bw[...], bm[...], bv[...], table.T[0:4], BIAS_RATE, power_one, power_two)
+    bw_out[...], bm_out[...], bv_out[...] = w, m, v
+    bl_out[...] = w.astype(BF)
+    for i in range(2, len(blocks)):
+        block(i)
+    for copy in stores:
+        copy.wait()
+
+
+def finish(lo, gio, cot, gco, gw, conv, proj, bias):
+    clips, r, slot = gio.shape
+    taps = conv[0].shape[2]
+    span = 2048
+    count = clips * (slot // span)
+    any_spec = pl.BlockSpec(memory_space=pltpu.HBM)
+    vmem = pl.BlockSpec(memory_space=pltpu.VMEM)
+    dma = pltpu.SemaphoreType.DMA
+
+    def like(a, dtype=None):
+        return jax.ShapeDtypeStruct(a.shape, dtype or a.dtype)
+
+    trio = [like(conv[0]), like(proj[0]), like(bias[0])]
+    return pl.pallas_call(
+        functools.partial(finish_kernel, taps, span),
+        out_shape=[like(lo), like(gio, F32), like(gco, F32)] + trio * 3
+        + [like(a, BF) for a in (conv[0], proj[0], bias[0])],
+        in_specs=[any_spec] * 11 + [vmem] * 3,
+        out_specs=[any_spec] * 3 + [any_spec, any_spec, vmem] * 4,
+        scratch_shapes=[
+            pltpu.VMEM(lo.shape, BF),
+            pltpu.VMEM(gio.shape, BF),
+            pltpu.VMEM(gio.shape, BF),
+            pltpu.VMEM(gio.shape, F32),
+            pltpu.VMEM(gco.shape, BF),
+            pltpu.VMEM(gco.shape, F32),
+            pltpu.VMEM(gw.shape, BF),
+            pltpu.VMEM((3, *conv[0].shape), F32),
+            pltpu.VMEM(conv[0].shape, BF),
+            pltpu.VMEM((3, *proj[0].shape), F32),
+            pltpu.VMEM(proj[0].shape, BF),
+            dma((count,)),
+            dma((count,)),
+            dma((count,)),
+            dma((8,)),
+            dma((2 * count + 9,)),
+        ],
+        compiler_params=pltpu.CompilerParams(vmem_limit_bytes=24 << 20),
+    )(lo, gio, cot, gco, gw, *conv, *proj, *bias)
+
+
 def per_device(
     n, d,
     inputs, conditioning, lengths, cotangent, conv_weight, out_weight, biases,
     conv_first, out_first, bias_first, conv_second, out_second, bias_second,
 ):
-    clips, r, slot = inputs.shape
-    taps = conv_weight.shape[0]
-    bias_low = biases.astype(BF)
-    flipped = jnp.transpose(conv_weight.astype(BF), (1, 2, 0))
-    flipped = jnp.concatenate(
-        [flipped, bias_low[0:2, :, None], jnp.zeros((2, r, KP - taps - 1), BF)], axis=2
-    )
-    out_low = out_weight.astype(BF).reshape(r, 2, 2, HALF)
-    wcat = jnp.stack(
-        [
-            jnp.concatenate(
-                [
-                    flipped[0],
-                    flipped[1],
-                    out_low[:, 0, side],
-                    out_low[:, 1, side],
-                    bias_low[2:4].T,
-                    jnp.zeros((r, WIDE - USED - 2), BF),
-                ],
-                axis=1,
-            )
-            for side in range(2)
-        ],
-        axis=0,
-    )
+    conv = [jnp.transpose(a, (1, 2, 0)) for a in (conv_weight, conv_first, conv_second)]
+    proj = [out_weight, out_first, out_second]
+    bias = [biases, bias_first, bias_second]
     cond = jnp.transpose(conditioning, (0, 2, 1))
-    layer_out, gio, gco, gw = run_layer(n, d, inputs, cotangent, cond, lengths, wcat)
-
-    grad_input = cotangent[:, 0].astype(F32) + gio.astype(F32)
-    grad_cond = jnp.transpose(gco.astype(F32), (0, 2, 1))
-    gsum = gw[0].astype(F32)
-    both = gsum[:, USED : USED + 2] + gw[1, :, USED : USED + 2].astype(F32)
-    conv_grad = jnp.transpose(
-        jnp.stack([gsum[:, :taps], gsum[:, KP : KP + taps]], axis=0), (2, 0, 1)
-    )
-    out_grad = jnp.stack(
-        [gw[:, :, OUT_AT : OUT_AT + HALF], gw[:, :, OUT_AT + HALF : USED]], axis=0
-    )
-    out_grad = jnp.transpose(out_grad, (2, 0, 1, 3)).reshape(r, 4 * HALF).astype(F32)
-    bias_grad = jnp.stack(
-        [gsum[:, taps], gsum[:, KP + taps], both[:, 0], both[:, 1]], axis=0
-    )
-    power_one = jnp.float32(BETA_ONE**STEP)
-    power_two = jnp.float32(BETA_TWO**STEP)
-    conv_new = adamw(
-        conv_weight, conv_first, conv_second, conv_grad, CONV_RATE, power_one, power_two
-    )
-    out_new = adamw(out_weight, out_first, out_second, out_grad, OUT_RATE, power_one, power_two)
-    bias_new = adamw(biases, bias_first, bias_second, bias_grad, BIAS_RATE, power_one, power_two)
-    return (
-        layer_out,
-        grad_input,
-        grad_cond,
-        conv_new[0],
-        out_new[0],
-        bias_new[0],
-        conv_new[1],
-        out_new[1],
-        bias_new[1],
-        conv_new[2],
-        out_new[2],
-        bias_new[2],
-        conv_new[0].astype(BF),
-        out_new[0].astype(BF),
-        bias_new[0].astype(BF),
-    )
+    lo, gio, gco, gw = run_layer(n, d, inputs, cotangent, cond, lengths, conv[0], proj[0], bias[0])
+    outs = finish(lo, gio, cotangent, gco, gw, conv, proj, bias)
+    layer_out, grad_input, grad_cond = outs[:3]
+    news = [jnp.transpose(a, (2, 0, 1)) if i % 3 == 0 else a for i, a in enumerate(outs[3:])]
+    return (layer_out, grad_input, jnp.transpose(grad_cond, (0, 2, 1)), *news)
 
 
 def solution(mesh):

time: 256 us -> 251 us (0.980)
  other arithmetic: 12.9 us -> 0 us
  Pallas kernels: 235 us -> 241 us
    pallas_call x0 -> x1, Pallas kernels: none -> 6.73 us  [finish(): pl.pallas_call(functools.partial(finish_kernel, taps, span), out_shape=[l...]
    convert_element_type x7 -> x0, other arithmetic: 5.01 us -> none  [the longest x1 1.62 us: per_device(): conv_new[0].astype(BF)]
    add x2 -> x0, other arithmetic: 4.91 us -> none  [the longest x1 4.91 us: per_device(): grad_input = cotangent[:, 0].astype(F32) + gio.astype(F32)]
    unnamed x24 -> x28, local copies, waits for them, and re-layouts: 4.81 us -> 8.1 us
where the time goes in v4:
time: 251 us; the launch traced here: 250 us
  Pallas kernels  241 us (96%)
  local copies, waits for them, and re-layouts  8.1 us (3%)
    pallas_call x1, Pallas kernels, run_layer(): pl.pallas_call(functools.partial(layer_kernel, n, d, clips, slot, sub, me...  235 us
    unnamed x28, local copies, waits for them, and re-layouts  8.1 us
    pallas_call x1, Pallas kernels, finish(): pl.pallas_call(functools.partial(finish_kernel, taps, span), out_shape=[l...  6.73 us

profile of v4, /device:TPU:0, one launch (start us, length us, event | category | flops | bytes accessed | tf_op | source)
XLA Modules:
  0.0 250.2 jit_solution(983087993733828134)
XLA Ops:
  0.7 0.0 copy-start.11
  0.7 0.0 copy-start.4
  0.7 0.0 copy-start.13
  0.7 0.0 copy-start.10
  0.7 0.0 copy-start.7
  0.7 0.0 copy-start.12
  0.7 0.0 copy-start.9
  0.7 0.0 copy-start.6
  0.7 0.0 copy-start.2
  0.7 234.6 %shard_map.244 = (bf16[2,2,64,8192]{3,2,1,0:T(8,128)(2,1)}, bf16[2,64,8192]{2,1,0:T(8,128)(2,1)}, bf16[2,80,1024]{2,1,0:T(8,128)(2,1)}, bf16[2,64,3072]{2,1,0:T(8,128)(2,1)}) custom-call(bf16[2,64,8192]{2,1,0:T(8,128)(2,1)} %x.1, bf16[2,2,64,8192]{3,2,1,0:T(8,128)(2,1)} %cot.3, bf16[2,80,1024]{2,1,0:T(8,128)(2,1)} %bitcast.13, s32[2]{0:T(128)} %lens.1, ...), custom_call_target="tpu_custom_call" | custom-call | tf_op jit(solution)/shard_map/pallas_call | solution.py:637
  235.3 0.0 copy-done.11
  235.3 0.0 copy-done.4
  235.3 0.0 copy-done.13
  235.3 0.0 copy-done.10
  235.4 0.0 copy-done.7
  235.4 0.0 copy-done.12
  235.4 0.0 copy-done.9
  235.4 0.0 copy-done.6
  235.4 0.0 copy-done.2
  235.4 0.0 copy-start
  235.4 2.2 copy-done
  237.6 0.0 copy-start.1
  237.6 2.2 copy-done.1
  239.8 0.0 copy-start.3
  239.8 1.6 copy-done.3
  241.4 0.0 copy-start.5
  241.4 1.1 copy-done.5
  242.5 0.0 copy-start.8
  242.5 1.0 copy-done.8
  243.5 6.7 %shard_map.245 = (bf16[2,2,64,8192]{3,2,1,0:T(8,128)(2,1)}, f32[2,64,8192]{2,1,0:T(8,128)}, f32[2,80,1024]{2,1,0:T(8,128)}, f32[2,64,1104]{2,1,0:T(8,128)}, f32[...) custom-call(bf16[2,2,64,8192]{3,2,1,0:T(8,128)(2,1)S(1)} %copy-done., ...), custom_call_target="tpu_custom_call" | custom-call | tf_op jit(solution)/shard_map/pallas_call | solution.py:821
Async XLA Ops:
  0.7 234.7 %copy-start.11 = (f32[4,64]{1,0:T(4,128)S(1)}, f32[4,64]{1,0:T(4,128)}, u32[]{:S(2)}) copy-start(f32[4,64]{1,0:T(4,128)} %bw.1) | copy-start | bytes 3076
  0.7 234.7 %copy-start.4 = (f32[64,1024]{1,0:T(8,128)S(1)}, f32[64,1024]{1,0:T(8,128)}, u32[]{:S(2)}) copy-start(f32[64,1024]{1,0:T(8,128)} %ow.1) | copy-start | bytes 786436
  0.7 234.7 %copy-start.13 = (f32[4,64]{1,0:T(4,128)S(1)}, f32[4,64]{1,0:T(4,128)}, u32[]{:S(2)}) copy-start(f32[4,64]{1,0:T(4,128)} %bv.1) | copy-start | bytes 3076
  0.7 234.7 %copy-start.10 = (f32[64,1024]{1,0:T(8,128)S(1)}, f32[64,1024]{1,0:T(8,128)}, u32[]{:S(2)}) copy-start(f32[64,1024]{1,0:T(8,128)} %ov.1) | copy-start | bytes 786436
  0.7 234.7 %copy-start.7 = (f32[1104,2,64]{0,2,1:T(8,128)S(1)}, f32[1104,2,64]{0,2,1:T(8,128)}, u32[]{:S(2)}) copy-start(f32[1104,2,64]{0,2,1:T(8,128)} %param.23) | copy-start | bytes 1695748
  0.7 234.7 %copy-start.12 = (f32[4,64]{1,0:T(4,128)S(1)}, f32[4,64]{1,0:T(4,128)}, u32[]{:S(2)}) copy-start(f32[4,64]{1,0:T(4,128)} %bm.1) | copy-start | bytes 3076
  0.7 234.7 %copy-start.9 = (f32[64,1024]{1,0:T(8,128)S(1)}, f32[64,1024]{1,0:T(8,128)}, u32[]{:S(2)}) copy-start(f32[64,1024]{1,0:T(8,128)} %om.1) | copy-start | bytes 786436
  0.7 234.7 %copy-start.6 = (f32[1104,2,64]{0,2,1:T(8,128)S(1)}, f32[1104,2,64]{0,2,1:T(8,128)}, u32[]{:S(2)}) copy-start(f32[1104,2,64]{0,2,1:T(8,128)} %param.20) | copy-start | bytes 1695748
  0.7 234.7 %copy-start.2 = (f32[1104,2,64]{0,2,1:T(8,128)S(1)}, f32[1104,2,64]{0,2,1:T(8,128)}, u32[]{:S(2)}) copy-start(f32[1104,2,64]{0,2,1:T(8,128)} %param.17) | copy-start | bytes 1695748
  235.4 2.2 copy-start
  237.6 2.2 copy-start.1
  239.8 1.6 copy-start.3
  241.4 1.1 copy-start.5
  242.5 1.0 copy-start.8

commit v5 on v4

--- a/solution.py
+++ b/solution.py
@@ -842,7 +842,7 @@
             dma((8,)),
             dma((2 * count + 9,)),
         ],
-        compiler_params=pltpu.CompilerParams(vmem_limit_bytes=24 << 20),
+        compiler_params=pltpu.CompilerParams(vmem_limit_bytes=60 << 20),
     )(lo, gio, cot, gco, gw, *conv, *proj, *bias)
 
 

time: 251 us -> 245 us (0.976)
  local copies, waits for them, and re-layouts: 8.1 us -> 0 us
  Pallas kernels: 241 us -> 244 us
    unnamed x28 -> x0, local copies, waits for them, and re-layouts: 8.1 us -> none
    pallas_call x1, Pallas kernels: 6.73 us -> 9.93 us  [finish(): pl.pallas_call(functools.partial(finish_kernel, taps, span), out_shape=[l...]
where the time goes in v5:
time: 245 us
  Pallas kernels  244 us (100%)
    pallas_call x1, Pallas kernels, run_layer(): pl.pallas_call(functools.partial(layer_kernel, n, d, clips, slot, sub, me...  234 us
    pallas_call x1, Pallas kernels, finish(): pl.pallas_call(functools.partial(finish_kernel, taps, span), out_shape=[l...  9.93 us

profile of v5, /device:TPU:0, one launch (start us, length us, event | category | flops | bytes accessed | tf_op | source)
XLA Modules:
  0.0 245.0 jit_solution(12732261522058375225)
XLA Ops:
  0.6 234.4 %shard_map.244 = (bf16[2,2,64,8192]{3,2,1,0:T(8,128)(2,1)}, bf16[2,64,8192]{2,1,0:T(8,128)(2,1)}, bf16[2,80,1024]{2,1,0:T(8,128)(2,1)}, bf16[2,64,3072]{2,1,0:T(8,128)(2,1)}) custom-call(bf16[2,64,8192]{2,1,0:T(8,128)(2,1)} %x.1, bf16[2,2,64,8192]{3,2,1,0:T(8,128)(2,1)} %cot.3, bf16[2,80,1024]{2,1,0:T(8,128)(2,1)} %bitcast.13, s32[2]{0:T(128)} %lens.1, ...), custom_call_target="tpu_custom_call" | custom-call | tf_op jit(solution)/shard_map/pallas_call | solution.py:637
  235.0 9.9 %shard_map.245 = (bf16[2,2,64,8192]{3,2,1,0:T(8,128)(2,1)}, f32[2,64,8192]{2,1,0:T(8,128)}, f32[2,80,1024]{2,1,0:T(8,128)}, f32[2,64,1104]{2,1,0:T(8,128)}, f32[...) custom-call(bf16[2,2,64,8192]{3,2,1,0:T(8,128)(2,1)} %get-tuple-elem, ...), custom_call_target="tpu_custom_call" | custom-call | tf_op jit(solution)/shard_map/pallas_call | solution.py:821

commit v6 on v4

--- a/solution.py
+++ b/solution.py
@@ -51,7 +51,7 @@
     n, d, clips, slot, sub, mel,
     x, cot, cond, lens, conv, proj, bias,
     bro, gio, gco, gw,
-    convf, turn, xin, cin, cnd, grecv, gsend, gown, wall, wtr, pg, gacc, csum, ost, gfs, gk, kr, r0, r1, s2, r2,
+    convf, turn, xin, cin, cnd, grecv, lay, wall, wtr, pg, gacc, csum, ost, gfs, gk, kr, r0, r1, s2, r2,
     sem_fx, sem_fc, sem_send, sem_xh, sem_xm, sem_c, sem_k, sem_km, sem_kr, sem_gm, sem_gv, sem_o, sem_gf, sem_in, sem_r1, sem_pre,
 ):
     g = lax.axis_index("dp")
@@ -127,10 +127,10 @@
     mine = lane(g * piece, piece)
 
     def laid(hh):
-        return gsend.at[rows(hh), pl.ds(0, WIDE)]
+        return lay.at[rows(hh), :]
 
     def laid_piece(hh):
-        return gsend.at[rows(hh), mine]
+        return lay.at[rows(hh), mine]
     kept = pl.ds(pl.multiple_of(wc * band, band), band)
 
     def send_cond(s):
@@ -308,7 +308,7 @@
 
         @pl.when(jnp.logical_not(hub))
         def _():
-            drain(gsend.at[pl.ds(0, 2 * r), mine], sem_send.at[1])
+            drain(lay.at[:, mine], sem_send.at[1])
 
 
         @pl.loop(0, USED // LANES)
@@ -329,10 +329,10 @@
                     + dot(tap(0), pe[0:512]) + dot(wtr[pl.ds(pl.multiple_of(KP + top, LANES), HALF), :], pe[512:1024]))
 
         def gone(q):
-            drain(gsend.at[:, pl.ds(0, sub)], sem_gv.at[lax.rem(q, POSTS)])
+            drain(cin.at[1, :, pl.ds(0, sub)], sem_gv.at[lax.rem(q, POSTS)])
 
         def give(q):
-            remote(gsend.at[:, lane((q + 1) * sub)], grecv.at[:, lane(q * sub)],
+            remote(cin.at[1, :, lane(q * sub)], grecv.at[:, lane(q * sub)],
                    sem_gv.at[lax.rem(q, POSTS)], sem_gm.at[q], g, mirror).start()
 
         def add_cond(s):
@@ -359,7 +359,7 @@
             def _():
                 drain(gfs.at[z], sem_gf.at[z])
 
-            gfs[z] = (gown[:, lane((q + 1) * sub)].astype(F32) + grecv[:, now].astype(F32)).astype(BF)
+            gfs[z] = (cin[0, :, now].astype(F32) + grecv[:, now].astype(F32)).astype(BF)
 
             @others
             def _(i):
@@ -458,15 +458,16 @@
             gacc[:, KP + 1024:OUT_AT] += dot_nt(pgg, cd)
             gacc[:, OUT_AT:USED] += dot_nt(hid, ct)
             gk[:, now] = (dot(wtr[1024:KP, :], pgf) + dot(wtr[KP + 1024:OUT_AT, :], pgg))[0:mel].astype(BF)
-            gsend[:, now] = back((1 - h) * HALF).astype(BF)
-            gown[:, now] = back(h * HALF).astype(BF)
+            before = lane(jnp.maximum(s - 1, 0) * sub)
+            cin[1, :, before] = back((1 - h) * HALF).astype(BF)
+            cin[0, :, before] = back(h * HALF).astype(BF)
             pg[0:512, 0:sub] = pgf
             pg[512:1024, 0:sub] = pgg
 
         send_results(blocks - 1)
         pg[:, sub:] = jnp.zeros((2 * GH, LANES), BF)
-        gsend[:, pl.ds(slot, sub)] = back((1 - h) * HALF).astype(BF)
-        gown[:, pl.ds(slot, sub)] = back(h * HALF).astype(BF)
+        cin[1, :, pl.ds(slot - sub, sub)] = back((1 - h) * HALF).astype(BF)
+        cin[0, :, pl.ds(slot - sub, sub)] = back(h * HALF).astype(BF)
 
         def spread(part, dst, sem):
             @others
@@ -479,7 +480,8 @@
         total = jnp.sum(csum[...], axis=1, keepdims=True)
         gacc[here, USED:USED + LANES] = jnp.where(spot == 0, total[0:HALF], jnp.where(spot == 1, total[HALF:], 0.0))
 
-        s0 = cin.at[0, :, pl.ds(0, WIDE)]
+        drain(xin.at[pl.ds(0, HALF - clips * r), pl.ds(0, slot)], sem_send.at[5])
+        s0 = xin.at[pl.ds(0, band), pl.ds(0, WIDE)]
         for k in range(1, clips):
             to = lax.rem(wc + k, clips)
             s0[...] = gacc[pl.ds(pl.multiple_of(to * band, band), band), :].astype(BF)
@@ -506,7 +508,7 @@
         @pl.loop(1, d)
         def _(k):
             to = lax.rem(g + k, d)
-            src = cin.at[1, :, lane((k - 1) * piece, piece)]
+            src = xin.at[pl.ds(GH - band, band), lane((k - 1) * piece, piece)]
             src[...] = gacc[kept, lane(to * piece, piece)].astype(BF)
             remote(src, r1.at[k - 1], sem_send.at[10], sem_r1.at[k - 1], to, m).start()
 
@@ -551,7 +553,6 @@
 
         drain(x.at[pl.ds(0, clips - 1)], sem_send.at[3])
         drain(cot.at[pl.ds(0, clips - 1)], sem_send.at[4])
-        drain(xin.at[pl.ds(0, HALF - clips * r), pl.ds(0, slot)], sem_send.at[5])
         drain(x, sem_send.at[17])
         drain(wall.at[kept, pl.ds(0, (d - 1) * piece)], sem_send.at[6])
         drain(wall.at[pl.ds(0, GH - band), :], sem_send.at[7])
@@ -603,7 +604,7 @@
         far()
         share_out()
         drain(cond, sem_send.at[0])
-        drain(gsend.at[pl.ds(0, 2 * r), mine], sem_send.at[1])
+        drain(lay.at[:, mine], sem_send.at[1])
         drain(bro, sem_in.at[10])
         drain(gio, sem_in.at[5])
         drain(gco, sem_in.at[6])
@@ -643,7 +644,7 @@
             jax.ShapeDtypeStruct((2, r, WIDE), BF),
         ),
         in_specs=[any_spec, any_spec, any_spec, smem, any_spec, any_spec, vmem],
-        out_specs=(any_spec, any_spec, any_spec, vmem),
+        out_specs=(pl.BlockSpec(memory_space=pl.ANY),) * 3 + (vmem,),
         scratch_shapes=[
             pltpu.VMEM(conv.shape, F32),
             pltpu.VMEM((8, LANES), F32),
@@ -651,8 +652,7 @@
             pltpu.VMEM((2, HALF, slot), BF),
             pltpu.VMEM((LANES, slot), BF),
             pltpu.VMEM((HALF, slot), BF),
-            pltpu.VMEM((HALF, slot + sub), BF),
-            pltpu.VMEM((HALF, slot + sub), BF),
+            pltpu.VMEM((2 * r, WIDE), BF),
             pltpu.VMEM((GH, WIDE), BF),
             pltpu.VMEM((USED, GH), BF),
             pltpu.VMEM((2 * GH, sub + LANES), BF),
@@ -684,7 +684,7 @@
             dma((2,)),
         ],
         compiler_params=pltpu.CompilerParams(
-            collective_id=0, has_side_effects=True, vmem_limit_bytes=60 << 20
+            collective_id=0, has_side_effects=True, vmem_limit_bytes=52 << 20
         ),
     )(x, cot, cond, lens, conv, proj, bias)
 
@@ -855,7 +855,13 @@
     proj = [out_weight, out_first, out_second]
     bias = [biases, bias_first, bias_second]
     cond = jnp.transpose(conditioning, (0, 2, 1))
-    lo, gio, gco, gw = run_layer(n, d, inputs, cotangent, cond, lengths, conv[0], proj[0], bias[0])
+    def pinned(a):
+        return pltpu.with_memory_space_constraint(a, pltpu.HBM)
+
+    lo, gio, gco, gw = run_layer(
+        n, d, pinned(inputs), pinned(cotangent), pinned(cond), pinned(lengths), pinned(conv[0]), pinned(proj[0]), pinned(bias[0])
+    )
+    lo, gio = pinned(lo), pinned(gio)
     outs = finish(lo, gio, cotangent, gco, gw, conv, proj, bias)
     layer_out, grad_input, grad_cond = outs[:3]
     news = [jnp.transpose(a, (2, 0, 1)) if i % 3 == 0 else a for i, a in enumerate(outs[3:])]

time: 251 us -> 242 us (0.964)
  local copies, waits for them, and re-layouts: 8.1 us -> 0.04 us
    unnamed x28 -> x20, local copies, waits for them, and re-layouts: 8.1 us -> 0.04 us
where the time goes in v6:
time: 242 us
  Pallas kernels  241 us (100%)
    pallas_call x1, Pallas kernels, run_layer(): pl.pallas_call(functools.partial(layer_kernel, n, d, clips, slot, sub, me...  234 us
    pallas_call x1, Pallas kernels, finish(): pl.pallas_call(functools.partial(finish_kernel, taps, span), out_shape=[l...  7.47 us

profile of v6, /device:TPU:0, one launch (start us, length us, event | category | flops | bytes accessed | tf_op | source)
XLA Modules:
  0.0 242.0 jit_solution(12055343144193281034)
XLA Ops:
  0.7 0.0 copy-start.7
  0.7 0.0 copy-start.2
  0.7 0.0 copy-start
  0.7 0.0 copy-start.9
  0.7 0.0 copy-start.6
  0.7 0.0 copy-start.4
  0.7 0.0 copy-start.8
  0.7 0.0 copy-start.5
  0.7 0.0 copy-start.3
  0.7 0.0 copy-start.1
  0.8 233.7 %shard_map.244 = (bf16[2,2,64,8192]{3,2,1,0:T(8,128)(2,1)}, bf16[2,64,8192]{2,1,0:T(8,128)(2,1)}, bf16[2,80,1024]{2,1,0:T(8,128)(2,1)S(1)}, bf16[2,64,3072]{2,1,0:T(8,128)(2,1)S(1)}) custom-call(bf16[2,64,8192]{2,1,0:T(8,128)(2,1)} %x.1, bf16[2,2,64,8192]{3,2,1,0:T(8,128)(2,1)} %cot.3, bf16[2,80,1024]{2,1,0:T(8,128)(2,1)} %bitcast.13, s32[2]{0:T(128)} %lens.1, ...), custom_call_target="tpu_custom_call" | custom-call | tf_op jit(solution)/shard_map/pallas_call | solution.py:638
  234.4 0.0 copy-done.7
  234.4 0.0 copy-done.2
  234.4 0.0 copy-done
  234.4 0.0 copy-done.9
  234.5 0.0 copy-done.6
  234.5 0.0 copy-done.4
  234.5 0.0 copy-done.8
  234.5 0.0 copy-done.5
  234.5 0.0 copy-done.3
  234.5 0.0 copy-done.1
  234.5 7.5 %shard_map.245 = (bf16[2,2,64,8192]{3,2,1,0:T(8,128)(2,1)}, f32[2,64,8192]{2,1,0:T(8,128)}, f32[2,80,1024]{2,1,0:T(8,128)}, f32[2,64,1104]{2,1,0:T(8,128)}, f32[...) custom-call(bf16[2,2,64,8192]{3,2,1,0:T(8,128)(2,1)} %get-tuple-elem, ...), custom_call_target="tpu_custom_call" | custom-call | tf_op jit(solution)/shard_map/pallas_call | solution.py:821
Async XLA Ops:
  0.7 233.8 %copy-start.7 = (f32[4,64]{1,0:T(4,128)S(1)}, f32[4,64]{1,0:T(4,128)}, u32[]{:S(2)}) copy-start(f32[4,64]{1,0:T(4,128)} %bw.1) | copy-start | bytes 3076
  0.7 233.8 %copy-start.2 = (f32[64,1024]{1,0:T(8,128)S(1)}, f32[64,1024]{1,0:T(8,128)}, u32[]{:S(2)}) copy-start(f32[64,1024]{1,0:T(8,128)} %ow.1) | copy-start | bytes 786436
  0.7 233.8 %copy-start = (bf16[2,2,64,8192]{3,2,1,0:T(8,128)(2,1)S(1)}, bf16[2,2,64,8192]{3,2,1,0:T(8,128)(2,1)}, u32[]{:S(2)}) copy-start(bf16[2,2,64,8192]{3,2,1,0:T(8,128)(2,1)} %cot.3) | copy-start | bytes 12582916
  0.7 233.8 %copy-start.9 = (f32[4,64]{1,0:T(4,128)S(1)}, f32[4,64]{1,0:T(4,128)}, u32[]{:S(2)}) copy-start(f32[4,64]{1,0:T(4,128)} %bv.1) | copy-start | bytes 3076
  0.7 233.8 %copy-start.6 = (f32[64,1024]{1,0:T(8,128)S(1)}, f32[64,1024]{1,0:T(8,128)}, u32[]{:S(2)}) copy-start(f32[64,1024]{1,0:T(8,128)} %ov.1) | copy-start | bytes 786436
  0.7 233.8 %copy-start.4 = (f32[1104,2,64]{0,2,1:T(8,128)S(1)}, f32[1104,2,64]{0,2,1:T(8,128)}, u32[]{:S(2)}) copy-start(f32[1104,2,64]{0,2,1:T(8,128)} %param.23) | copy-start | bytes 1695748
  0.7 233.8 %copy-start.8 = (f32[4,64]{1,0:T(4,128)S(1)}, f32[4,64]{1,0:T(4,128)}, u32[]{:S(2)}) copy-start(f32[4,64]{1,0:T(4,128)} %bm.1) | copy-start | bytes 3076
  0.7 233.8 %copy-start.5 = (f32[64,1024]{1,0:T(8,128)S(1)}, f32[64,1024]{1,0:T(8,128)}, u32[]{:S(2)}) copy-start(f32[64,1024]{1,0:T(8,128)} %om.1) | copy-start | bytes 786436
  0.7 233.8 %copy-start.3 = (f32[1104,2,64]{0,2,1:T(8,128)S(1)}, f32[1104,2,64]{0,2,1:T(8,128)}, u32[]{:S(2)}) copy-start(f32[1104,2,64]{0,2,1:T(8,128)} %param.20) | copy-start | bytes 1695748
  0.7 233.8 %copy-start.1 = (f32[1104,2,64]{0,2,1:T(8,128)S(1)}, f32[1104,2,64]{0,2,1:T(8,128)}, u32[]{:S(2)}) copy-start(f32[1104,2,64]{0,2,1:T(8,128)} %param.17) | copy-start | bytes 1695748

commit v7 on v6

--- a/solution.py
+++ b/solution.py
@@ -31,7 +31,7 @@
 OWN = 6
 DIRECT = 6
 GIVE = 14
-LAG = 8
+LAG = 6
 SLOTS = 4
 LATE = 12
 POSTS = 8
@@ -212,9 +212,9 @@
                 remote(cot.at[c, :, :, lane(at)], cin.at[:, rows(local), lane(at)],
                        sem_fc.at[lax.rem(s, SLOTS)], sem_c.at[s], g, wid(h, c)).start()
 
-        pl.loop(0, 2)(send_x)
+        pl.loop(0, 1)(send_x)
         weights()
-        pl.loop(2, AHEAD)(send_x)
+        pl.loop(1, AHEAD)(send_x)
 
         @pl.loop(0, blocks)
         def _(s):

time: 242 us -> 241 us (level)
  no operation moved by 1% of the time
where the time goes in v7:
time: 241 us
  Pallas kernels  240 us (100%)
    pallas_call x1, Pallas kernels, run_layer(): pl.pallas_call(functools.partial(layer_kernel, n, d, clips, slot, sub, me...  232 us
    pallas_call x1, Pallas kernels, finish(): pl.pallas_call(functools.partial(finish_kernel, taps, span), out_shape=[l...  7.47 us

profile of v7, /device:TPU:0, one launch (start us, length us, event | category | flops | bytes accessed | tf_op | source)
XLA Modules:
  0.0 240.6 jit_solution(741258870653230953)
XLA Ops:
  0.7 0.0 copy-start.7
  0.7 0.0 copy-start.2
  0.7 0.0 copy-start
  0.7 0.0 copy-start.9
  0.7 0.0 copy-start.6
  0.7 0.0 copy-start.4
  0.7 0.0 copy-start.8
  0.7 0.0 copy-start.5
  0.7 0.0 copy-start.3
  0.7 0.0 copy-start.1
  0.8 232.3 %shard_map.244 = (bf16[2,2,64,8192]{3,2,1,0:T(8,128)(2,1)}, bf16[2,64,8192]{2,1,0:T(8,128)(2,1)}, bf16[2,80,1024]{2,1,0:T(8,128)(2,1)S(1)}, bf16[2,64,3072]{2,1,0:T(8,128)(2,1)S(1)}) custom-call(bf16[2,64,8192]{2,1,0:T(8,128)(2,1)} %x.1, bf16[2,2,64,8192]{3,2,1,0:T(8,128)(2,1)} %cot.3, bf16[2,80,1024]{2,1,0:T(8,128)(2,1)} %bitcast.13, s32[2]{0:T(128)} %lens.1, ...), custom_call_target="tpu_custom_call" | custom-call | tf_op jit(solution)/shard_map/pallas_call | solution.py:638
  233.0 0.0 copy-done.7
  233.0 0.0 copy-done.2
  233.0 0.0 copy-done
  233.0 0.0 copy-done.9
  233.1 0.0 copy-done.6
  233.1 0.0 copy-done.4
  233.1 0.0 copy-done.8
  233.1 0.0 copy-done.5
  233.1 0.0 copy-done.3
  233.1 0.0 copy-done.1
  233.1 7.5 %shard_map.245 = (bf16[2,2,64,8192]{3,2,1,0:T(8,128)(2,1)}, f32[2,64,8192]{2,1,0:T(8,128)}, f32[2,80,1024]{2,1,0:T(8,128)}, f32[2,64,1104]{2,1,0:T(8,128)}, f32[...) custom-call(bf16[2,2,64,8192]{3,2,1,0:T(8,128)(2,1)} %get-tuple-elem, ...), custom_call_target="tpu_custom_call" | custom-call | tf_op jit(solution)/shard_map/pallas_call | solution.py:821
Async XLA Ops:
  0.7 232.4 %copy-start.7 = (f32[4,64]{1,0:T(4,128)S(1)}, f32[4,64]{1,0:T(4,128)}, u32[]{:S(2)}) copy-start(f32[4,64]{1,0:T(4,128)} %bw.1) | copy-start | bytes 3076
  0.7 232.4 %copy-start.2 = (f32[64,1024]{1,0:T(8,128)S(1)}, f32[64,1024]{1,0:T(8,128)}, u32[]{:S(2)}) copy-start(f32[64,1024]{1,0:T(8,128)} %ow.1) | copy-start | bytes 786436
  0.7 232.4 %copy-start = (bf16[2,2,64,8192]{3,2,1,0:T(8,128)(2,1)S(1)}, bf16[2,2,64,8192]{3,2,1,0:T(8,128)(2,1)}, u32[]{:S(2)}) copy-start(bf16[2,2,64,8192]{3,2,1,0:T(8,128)(2,1)} %cot.3) | copy-start | bytes 12582916
  0.7 232.4 %copy-start.9 = (f32[4,64]{1,0:T(4,128)S(1)}, f32[4,64]{1,0:T(4,128)}, u32[]{:S(2)}) copy-start(f32[4,64]{1,0:T(4,128)} %bv.1) | copy-start | bytes 3076
  0.7 232.4 %copy-start.6 = (f32[64,1024]{1,0:T(8,128)S(1)}, f32[64,1024]{1,0:T(8,128)}, u32[]{:S(2)}) copy-start(f32[64,1024]{1,0:T(8,128)} %ov.1) | copy-start | bytes 786436
  0.7 232.4 %copy-start.4 = (f32[1104,2,64]{0,2,1:T(8,128)S(1)}, f32[1104,2,64]{0,2,1:T(8,128)}, u32[]{:S(2)}) copy-start(f32[1104,2,64]{0,2,1:T(8,128)} %param.23) | copy-start | bytes 1695748
  0.7 232.4 %copy-start.8 = (f32[4,64]{1,0:T(4,128)S(1)}, f32[4,64]{1,0:T(4,128)}, u32[]{:S(2)}) copy-start(f32[4,64]{1,0:T(4,128)} %bm.1) | copy-start | bytes 3076
  0.7 232.4 %copy-start.5 = (f32[64,1024]{1,0:T(8,128)S(1)}, f32[64,1024]{1,0:T(8,128)}, u32[]{:S(2)}) copy-start(f32[64,1024]{1,0:T(8,128)} %om.1) | copy-start | bytes 786436
  0.7 232.4 %copy-start.3 = (f32[1104,2,64]{0,2,1:T(8,128)S(1)}, f32[1104,2,64]{0,2,1:T(8,128)}, u32[]{:S(2)}) copy-start(f32[1104,2,64]{0,2,1:T(8,128)} %param.20) | copy-start | bytes 1695748
  0.7 232.4 %copy-start.1 = (f32[1104,2,64]{0,2,1:T(8,128)S(1)}, f32[1104,2,64]{0,2,1:T(8,128)}, u32[]{:S(2)}) copy-start(f32[1104,2,64]{0,2,1:T(8,128)} %param.17) | copy-start | bytes 1695748

commit v8 on v7

--- a/solution.py
+++ b/solution.py
@@ -185,8 +185,8 @@
 
         @pl.when(jnp.logical_not(hub))
         def _():
+            remote(laid_piece(1 - h), s2.at[rows(local), :], sem_send.at[1], sem_in.at[3], g, wid(h, h)).start()
             remote(laid_piece(h), wall.at[rows(m), mine], sem_send.at[1], sem_in.at[0], g, wid(h, h)).start()
-            remote(laid_piece(1 - h), s2.at[rows(local), :], sem_send.at[1], sem_in.at[3], g, wid(h, h)).start()
 
     def far():
         def send_x(s):
@@ -282,12 +282,13 @@
         csum[...] = jnp.zeros_like(csum)
 
         pl.loop(0, 2)(relay)
-        drain(wall.at[kept, mine], sem_in.at[0])
 
         @pl.when(hub)
         def _():
             drain(s2, sem_in.at[3])
             remote(s2, wall.at[kept, mine], sem_send.at[2], sem_in.at[0], g, mirror).start()
+
+        drain(wall.at[kept, mine], sem_in.at[0])
 
         @pl.loop(1, d)
         def _(k):
@@ -684,7 +685,7 @@
             dma((2,)),
         ],
         compiler_params=pltpu.CompilerParams(
-            collective_id=0, has_side_effects=True, vmem_limit_bytes=52 << 20
+            collective_id=0, has_side_effects=True, vmem_limit_bytes=50 << 20
         ),
     )(x, cot, cond, lens, conv, proj, bias)
 
@@ -705,8 +706,8 @@
     lo, gio, cot, gco, gw, cw, cm, cv, ow, om, ov, bw, bm, bv,
     lo_out, gi_out, gc_out, cw_out, ow_out, bw_out, cm_out, om_out, bm_out, cv_out, ov_out, bv_out,
     cl_out, ol_out, bl_out,
-    lo_v, gio_v, cot_v, gi_v, gco_v, gc_v, gw_v, conv_v, convl_v, proj_v, projl_v,
-    sem_lo, sem_gi, sem_cot, sem_small, sem_out,
+    lo_v, gi_v, gco_v, gc_v, gw_v, conv_v, convl_v, proj_v, projl_v,
+    sem_lo, sem_small, sem_out,
 ):
     clips, r, slot = gio.shape
     parts = slot // span
@@ -717,15 +718,11 @@
         pltpu.make_async_copy(src, dst, sem_small.at[i])
         for i, (src, dst) in enumerate(
             [(gw, gw_v), (gco, gco_v)]
-            + [(a, conv_v.at[q]) for q, a in enumerate((cw, cm, cv))]
-            + [(a, proj_v.at[q]) for q, a in enumerate((ow, om, ov))]
         )
     ]
     blocks = [(c, slice(p * span, (p + 1) * span)) for c in range(clips) for p in range(parts)]
     loads = [
         (
-            pltpu.make_async_copy(gio.at[c, :, at], gio_v.at[c, :, at], sem_gi.at[i]),
-            pltpu.make_async_copy(cot.at[c, 0, :, at], cot_v.at[c, :, at], sem_cot.at[i]),
             pltpu.make_async_copy(lo.at[c, :, :, at], lo_v.at[c, :, :, at], sem_lo.at[i]),
         )
         for i, (c, at) in enumerate(blocks)
@@ -750,13 +747,10 @@
 
     def block(i):
         c, at = blocks[i]
-        one, two, three = loads[i]
-        three.wait()
+        gi_v[c, :, at] = cot[c, 0, :, at].astype(F32) + gio[c, :, at].astype(F32)
+        store(gi_v.at[c, :, at], gi_out.at[c, :, at])
+        loads[i][0].wait()
         store(lo_v.at[c, :, :, at], lo_out.at[c, :, :, at])
-        one.wait()
-        two.wait()
-        gi_v[c, :, at] = cot_v[c, :, at].astype(F32) + gio_v[c, :, at].astype(F32)
-        store(gi_v.at[c, :, at], gi_out.at[c, :, at])
 
     block(0)
     for copy in small[:5]:
@@ -764,7 +758,7 @@
     gc_v[...] = gco_v[...].astype(F32)
     store(gc_v, gc_out)
     for q in range(2):
-        w, m, v = adamw(conv_v[0, q], conv_v[1, q], conv_v[2, q], gw_v[0, :, q * KP:q * KP + taps].astype(F32),
+        w, m, v = adamw(cw[q], cm[q], cv[q], gw_v[0, :, q * KP:q * KP + taps].astype(F32),
                         CONV_RATE, power_one, power_two)
         conv_v[0, q], conv_v[1, q], conv_v[2, q] = w, m, v
         convl_v[q] = w.astype(BF)
@@ -777,7 +771,7 @@
     for q in range(4):
         at = slice(q * HALF, (q + 1) * HALF)
         from_at = OUT_AT + q // 2 * HALF
-        w, m, v = adamw(proj_v[0, :, at], proj_v[1, :, at], proj_v[2, :, at],
+        w, m, v = adamw(ow[:, at], om[:, at], ov[:, at],
                         gw_v[q % 2, :, from_at:from_at + HALF].astype(F32), OUT_RATE, power_one, power_two)
         proj_v[0, :, at], proj_v[1, :, at], proj_v[2, :, at] = w, m, v
         projl_v[:, at] = w.astype(BF)
@@ -822,12 +816,10 @@
         functools.partial(finish_kernel, taps, span),
         out_shape=[like(lo), like(gio, F32), like(gco, F32)] + trio * 3
         + [like(a, BF) for a in (conv[0], proj[0], bias[0])],
-        in_specs=[any_spec] * 11 + [vmem] * 3,
+        in_specs=[any_spec] + [vmem] * 2 + [any_spec] * 2 + [vmem] * 9,
         out_specs=[any_spec] * 3 + [any_spec, any_spec, vmem] * 4,
         scratch_shapes=[
             pltpu.VMEM(lo.shape, BF),
-            pltpu.VMEM(gio.shape, BF),
-            pltpu.VMEM(gio.shape, BF),
             pltpu.VMEM(gio.shape, F32),
             pltpu.VMEM(gco.shape, BF),
             pltpu.VMEM(gco.shape, F32),
@@ -837,9 +829,7 @@
             pltpu.VMEM((3, *proj[0].shape), F32),
             pltpu.VMEM(proj[0].shape, BF),
             dma((count,)),
-            dma((count,)),
-            dma((count,)),
-            dma((8,)),
+            dma((2,)),
             dma((2 * count + 9,)),
         ],
         compiler_params=pltpu.CompilerParams(vmem_limit_bytes=24 << 20),
@@ -861,7 +851,7 @@
     lo, gio, gco, gw = run_layer(
         n, d, pinned(inputs), pinned(cotangent), pinned(cond), pinned(lengths), pinned(conv[0]), pinned(proj[0]), pinned(bias[0])
     )
-    lo, gio = pinned(lo), pinned(gio)
+    lo = pinned(lo)
     outs = finish(lo, gio, cotangent, gco, gw, conv, proj, bias)
     layer_out, grad_input, grad_cond = outs[:3]
     news = [jnp.transpose(a, (2, 0, 1)) if i % 3 == 0 else a for i, a in enumerate(outs[3:])]

time: 241 us -> 240 us (level)
  no operation moved by 1% of the time
where the time goes in v8:
time: 240 us
  Pallas kernels  239 us (100%)
    pallas_call x1, Pallas kernels, run_layer(): pl.pallas_call(functools.partial(layer_kernel, n, d, clips, slot, sub, me...  232 us
    pallas_call x1, Pallas kernels, finish(): pl.pallas_call(functools.partial(finish_kernel, taps, span), out_shape=[l...  6.64 us

profile of v8, /device:TPU:0, one launch (start us, length us, event | category | flops | bytes accessed | tf_op | source)
XLA Modules:
  0.0 239.6 jit_solution(861483111355404500)
XLA Ops:
  0.7 0.0 copy-start.7
  0.7 0.0 copy-start.2
  0.7 0.0 copy-start
  0.7 0.0 copy-start.9
  0.7 0.0 copy-start.6
  0.7 0.0 copy-start.4
  0.7 0.0 copy-start.8
  0.7 0.0 copy-start.5
  0.7 0.0 copy-start.3
  0.7 0.0 copy-start.1
  0.8 232.1 %shard_map.244 = (bf16[2,2,64,8192]{3,2,1,0:T(8,128)(2,1)}, bf16[2,64,8192]{2,1,0:T(8,128)(2,1)S(1)}, bf16[2,80,1024]{2,1,0:T(8,128)(2,1)S(1)}, bf16[2,64,3072]{2,1,0:T(8,128)(2,1)S(1)}) custom-call(bf16[2,64,8192]{2,1,0:T(8,128)(2,1)} %x.1, bf16[2,2,64,8192]{3,2,1,0:T(8,128)(2,1)} %cot.3, bf16[2,80,1024]{2,1,0:T(8,128)(2,1)} %bitcast.13, s32[2]{0:T(128)} %lens.1, ...), custom_call_target="tpu_custom_call" | custom-call | tf_op jit(solution)/shard_map/pallas_call | solution.py:639
  232.9 0.0 copy-done.7
  232.9 0.0 copy-done.2
  232.9 0.0 copy-done
  232.9 0.0 copy-done.9
  232.9 0.0 copy-done.6
  233.0 0.0 copy-done.4
  233.0 0.0 copy-done.8
  233.0 0.0 copy-done.5
  233.0 0.0 copy-done.3
  233.0 0.0 copy-done.1
  233.0 6.6 %shard_map.245 = (bf16[2,2,64,8192]{3,2,1,0:T(8,128)(2,1)}, f32[2,64,8192]{2,1,0:T(8,128)}, f32[2,80,1024]{2,1,0:T(8,128)}, f32[2,64,1104]{2,1,0:T(8,128)}, f32[...) custom-call(bf16[2,2,64,8192]{3,2,1,0:T(8,128)(2,1)} %get-tuple-elem, ...), custom_call_target="tpu_custom_call" | custom-call | tf_op jit(solution)/shard_map/pallas_call | solution.py:815
Async XLA Ops:
  0.7 232.3 %copy-start.7 = (f32[4,64]{1,0:T(4,128)S(1)}, f32[4,64]{1,0:T(4,128)}, u32[]{:S(2)}) copy-start(f32[4,64]{1,0:T(4,128)} %bw.1) | copy-start | bytes 3076
  0.7 232.3 %copy-start.2 = (f32[64,1024]{1,0:T(8,128)S(1)}, f32[64,1024]{1,0:T(8,128)}, u32[]{:S(2)}) copy-start(f32[64,1024]{1,0:T(8,128)} %ow.1) | copy-start | bytes 786436
  0.7 232.3 %copy-start = (bf16[2,2,64,8192]{3,2,1,0:T(8,128)(2,1)S(1)}, bf16[2,2,64,8192]{3,2,1,0:T(8,128)(2,1)}, u32[]{:S(2)}) copy-start(bf16[2,2,64,8192]{3,2,1,0:T(8,128)(2,1)} %cot.3) | copy-start | bytes 12582916
  0.7 232.3 %copy-start.9 = (f32[4,64]{1,0:T(4,128)S(1)}, f32[4,64]{1,0:T(4,128)}, u32[]{:S(2)}) copy-start(f32[4,64]{1,0:T(4,128)} %bv.1) | copy-start | bytes 3076
  0.7 232.3 %copy-start.6 = (f32[64,1024]{1,0:T(8,128)S(1)}, f32[64,1024]{1,0:T(8,128)}, u32[]{:S(2)}) copy-start(f32[64,1024]{1,0:T(8,128)} %ov.1) | copy-start | bytes 786436
  0.7 232.3 %copy-start.4 = (f32[1104,2,64]{0,2,1:T(8,128)S(1)}, f32[1104,2,64]{0,2,1:T(8,128)}, u32[]{:S(2)}) copy-start(f32[1104,2,64]{0,2,1:T(8,128)} %param.23) | copy-start | bytes 1695748
  0.7 232.3 %copy-start.8 = (f32[4,64]{1,0:T(4,128)S(1)}, f32[4,64]{1,0:T(4,128)}, u32[]{:S(2)}) copy-start(f32[4,64]{1,0:T(4,128)} %bm.1) | copy-start | bytes 3076
  0.7 232.3 %copy-start.5 = (f32[64,1024]{1,0:T(8,128)S(1)}, f32[64,1024]{1,0:T(8,128)}, u32[]{:S(2)}) copy-start(f32[64,1024]{1,0:T(8,128)} %om.1) | copy-start | bytes 786436
  0.7 232.3 %copy-start.3 = (f32[1104,2,64]{0,2,1:T(8,128)S(1)}, f32[1104,2,64]{0,2,1:T(8,128)}, u32[]{:S(2)}) copy-start(f32[1104,2,64]{0,2,1:T(8,128)} %param.20) | copy-start | bytes 1695748
  0.7 232.3 %copy-start.1 = (f32[1104,2,64]{0,2,1:T(8,128)S(1)}, f32[1104,2,64]{0,2,1:T(8,128)}, u32[]{:S(2)}) copy-start(f32[1104,2,64]{0,2,1:T(8,128)} %param.17) | copy-start | bytes 1695748
